TPU v7x, 256 devices: a whole 4x4x8 slice. The times are simulated.
256 devices in a mesh: noise: 32 (over z, y), dp: 8 (over x, core).
Axes of the slice: x: 4, y: 4, z: 8, core: 2. Of those that a mesh axis runs over, the one named last changes fastest.
Arguments:
- noise_batch: bfloat16 [32768, 1024], P('noise', 'dp'), may hold values from -6 to 6
- latents: bfloat16 [16384, 1024], P('dp', 'noise'), may hold values from -6 to 6
Outputs:
- row_potential: float32 [32768], P('noise')
- col_potential: float32 [16384], P('dp')
- target: bfloat16 [32768, 1024], P('noise', 'dp')
All inputs are finite; a program needn't handle non-finite values.
Results may differ from a plain program's by a relative error of at most 0.015.
Values may be sent and summed in bfloat16 or wider, within the bound.
A program may use at most 64 MiB of HBM per device.

v0:
```python
import math

import jax
import jax.numpy as jnp
from jax import lax
from jax.sharding import PartitionSpec as P

ITERS = 3


epsilon = 0.01


def column_lse(scaled):
    peak_value = lax.pmax(jnp.max(scaled, axis=0), "noise")
    exp_total = lax.psum(jnp.sum(jnp.exp(scaled - peak_value[None, :]), axis=0), "noise")
    return peak_value + jnp.log(exp_total)


def row_lse(scaled):
    peak_value = lax.pmax(jnp.max(scaled, axis=1), "dp")
    exp_total = lax.psum(jnp.sum(jnp.exp(scaled - peak_value[:, None]), axis=1), "dp")
    return peak_value + jnp.log(exp_total)


def local(noise_batch, latents):
    rows_here = lax.all_gather(noise_batch, "dp", axis=1, tiled=True)
    feature_count = rows_here.shape[1]
    local_rows = rows_here.shape[0]
    local_cols = latents.shape[0]
    total_rows = local_rows * lax.axis_size("noise")
    total_cols = local_cols * lax.axis_size("dp")
    noise_f = rows_here.astype(jnp.float32)
    row_norms = jnp.sum(noise_f * noise_f, axis=1)
    full_latents = lax.all_gather(latents, "noise", axis=1, tiled=True)
    latent_f = full_latents.astype(jnp.float32)
    col_norms = jnp.sum(latent_f * latent_f, axis=1)
    cross_term = lax.dot_general(
        rows_here, full_latents, (((1,), (1,)), ((), ())), preferred_element_type=jnp.float32
    )
    cost_tile = (row_norms[:, None] + col_norms[None, :] - 2.0 * cross_term) / feature_count
    row_potential = jnp.zeros((local_rows,), jnp.float32)
    col_potential = jnp.zeros((local_cols,), jnp.float32)
    for step in range(ITERS):
        col_potential = -epsilon * math.log(total_cols) - epsilon * column_lse(
            (row_potential[:, None] - cost_tile) / epsilon
        )
        row_potential = -epsilon * math.log(total_rows) - epsilon * row_lse(
            (col_potential[None, :] - cost_tile) / epsilon
        )
    weights = jnp.exp(
        (row_potential[:, None] + col_potential[None, :] - cost_tile) / epsilon
        + math.log(total_rows)
    ).astype(jnp.bfloat16)
    numerator = jnp.dot(weights, full_latents, preferred_element_type=jnp.float32)
    target = lax.psum_scatter(numerator.astype(jnp.bfloat16), "dp", scatter_dimension=1, tiled=True)
    return (row_potential, col_potential, target)


def solution(mesh):
    in_specs = (P("noise", "dp"), P("dp", "noise"))
    out_specs = (P("noise"), P("dp"), P("noise", "dp"))
    return jax.shard_map(local, mesh=mesh, in_specs=in_specs, out_specs=out_specs, check_vma=False)
```

profile of v0, /device:TPU:1, one launch (start us, length us, event | category | flops | bytes accessed | tf_op | source)
XLA Modules:
  0.0 747.1 jit_solution(5696732393647302910)
XLA Ops:
  8.7 35.2 %all-gather.3.cloned.1.call-done = bf16[1024,1024]{1,0:T(8,128)(2,1)} async-done(((bf16[1024,128]{1,0:T(8,128)(2,1)}), bf16[1024,1024]{1,0:T(8,128)(2,1)}) %all-gather.3.cloned.1.call-update) | async-done | bytes 2097168 | tf_op jit(solution)/shard_map/all_gather | solution.py:27
  43.8 2.1 multiply_reduce_fusion.1
  45.9 80.4 %all-gather.5.cloned.1.call-done = bf16[2048,1024]{0,1:T(8,128)(2,1)} async-done(((bf16[2048,32]{0,1:T(8,128)(2,1)}), bf16[2048,1024]{0,1:T(8,128)(2,1)}) %all-gather.5.cloned.1.call-update) | async-done | bytes 4194320 | tf_op jit(solution)/shard_map/all_gather | solution.py:35
  126.3 3.1 multiply_reduce_fusion
  129.3 11.1 %fusion = (f32[2048]{0:T(1024)S(1)}, f32[1024,2048]{1,0:T(8,128)}) fusion(bf16[1024,1024]{1,0:T(8,128)(2,1)} %all-gather.3.cloned.1.call-done, bf16[2048,1024]{0,1:T(8,128)(2,1)} %all-gather.5.cloned.1.call-done, f32[2048]{0:T(1024)S(1)} %multiply_reduce_fusion, f32[1024]{0:T(1024)S(1)} %multiply_reduce_fusion.1), kind=kOutput, calls=%fused_computation.15 | convolution fusion | flops 4309645312 | bytes 14700544 | tf_op jit(solution)/shard_map/dot_general | solution.py:38
  140.5 58.5 %pmax.42 = f32[2048]{0:T(1024)S(1)} all-reduce(f32[2048]{0:T(1024)S(1)} %get-tuple-element.3), channel_id=1, replica_groups=mesh['noise'=32,'dp'=8] {'noise'}, use_global_device_ids=true, to_apply=%region_3.0 | all-reduce | flops 2048 | bytes 16384 | tf_op jit(solution)/shard_map/pmax | solution.py:15
  199.0 5.0 exponential_reduce_fusion.5
  204.0 56.8 %psum.42 = f32[2048]{0:T(1024)S(1)} all-reduce(f32[2048]{0:T(1024)S(1)} %exponential_reduce_fusion.5), channel_id=1, replica_groups=mesh['noise'=32,'dp'=8] {'noise'}, use_global_device_ids=true, to_apply=%region_5.0 | all-reduce | flops 2048 | bytes 16384 | tf_op jit(solution)/shard_map/psum | solution.py:16
  260.8 4.3 fusion.1
  265.1 44.0 %pmax.43 = f32[1024]{0:T(1024)S(1)} all-reduce(f32[1024]{0:T(1024)S(1)} %fusion.1), channel_id=1, replica_groups=mesh['noise'=32,'dp'=8] {'dp'}, use_global_device_ids=true, to_apply=%region_7.0 | all-reduce | flops 1024 | bytes 8192 | tf_op jit(solution)/shard_map/pmax | solution.py:21
  309.0 4.5 exponential_reduce_fusion.4
  313.5 12.4 %psum.43 = f32[1024]{0:T(1024)S(1)} all-reduce(f32[1024]{0:T(1024)S(1)} %exponential_reduce_fusion.4), channel_id=1, replica_groups=mesh['noise'=32,'dp'=8] {'dp'}, use_global_device_ids=true, to_apply=%region_9.0 | all-reduce | flops 1024 | bytes 8192 | tf_op jit(solution)/shard_map/psum | solution.py:22
  326.0 4.3 fusion.2
  330.3 59.1 %pmax.44 = f32[2048]{0:T(1024)S(1)} all-reduce(f32[2048]{0:T(1024)S(1)} %fusion.2), channel_id=1, replica_groups=mesh['noise'=32,'dp'=8] {'noise'}, use_global_device_ids=true, to_apply=%region_11.0 | all-reduce | flops 2048 | bytes 16384 | tf_op jit(solution)/shard_map/pmax | solution.py:15
  389.4 4.5 exponential_reduce_fusion.3
  393.9 57.2 %psum.44 = f32[2048]{0:T(1024)S(1)} all-reduce(f32[2048]{0:T(1024)S(1)} %exponential_reduce_fusion.3), channel_id=1, replica_groups=mesh['noise'=32,'dp'=8] {'noise'}, use_global_device_ids=true, to_apply=%region_13.0 | all-reduce | flops 2048 | bytes 16384 | tf_op jit(solution)/shard_map/psum | solution.py:16
  451.2 4.3 fusion.3
  455.4 39.6 %pmax.45 = f32[1024]{0:T(1024)S(1)} all-reduce(f32[1024]{0:T(1024)S(1)} %fusion.3), channel_id=1, replica_groups=mesh['noise'=32,'dp'=8] {'dp'}, use_global_device_ids=true, to_apply=%region_15.0 | all-reduce | flops 1024 | bytes 8192 | tf_op jit(solution)/shard_map/pmax | solution.py:21
  495.0 4.5 exponential_reduce_fusion.2
  499.5 12.4 %psum.45 = f32[1024]{0:T(1024)S(1)} all-reduce(f32[1024]{0:T(1024)S(1)} %exponential_reduce_fusion.2), channel_id=1, replica_groups=mesh['noise'=32,'dp'=8] {'dp'}, use_global_device_ids=true, to_apply=%region_17.0 | all-reduce | flops 1024 | bytes 8192 | tf_op jit(solution)/shard_map/psum | solution.py:22
  512.0 4.3 fusion.4
  516.3 59.2 %pmax.46 = f32[2048]{0:T(1024)S(1)} all-reduce(f32[2048]{0:T(1024)S(1)} %fusion.4), channel_id=1, replica_groups=mesh['noise'=32,'dp'=8] {'noise'}, use_global_device_ids=true, to_apply=%region_19.0 | all-reduce | flops 2048 | bytes 16384 | tf_op jit(solution)/shard_map/pmax | solution.py:15
  575.4 4.5 exponential_reduce_fusion.1
  579.9 57.0 %psum.46 = f32[2048]{0:T(1024)S(1)} all-reduce(f32[2048]{0:T(1024)S(1)} %exponential_reduce_fusion.1), channel_id=1, replica_groups=mesh['noise'=32,'dp'=8] {'noise'}, use_global_device_ids=true, to_apply=%region_21.0 | all-reduce | flops 2048 | bytes 16384 | tf_op jit(solution)/shard_map/psum | solution.py:16
  637.0 4.3 fusion.5
  641.3 39.6 %pmax.47 = f32[1024]{0:T(1024)S(1)} all-reduce(f32[1024]{0:T(1024)S(1)} %fusion.5), channel_id=1, replica_groups=mesh['noise'=32,'dp'=8] {'dp'}, use_global_device_ids=true, to_apply=%region_23.0 | all-reduce | flops 1024 | bytes 8192 | tf_op jit(solution)/shard_map/pmax | solution.py:21
  680.9 4.5 exponential_reduce_fusion
  685.4 12.4 %psum.47 = f32[1024]{0:T(1024)S(1)} all-reduce(f32[1024]{0:T(1024)S(1)} %exponential_reduce_fusion), channel_id=1, replica_groups=mesh['noise'=32,'dp'=8] {'dp'}, use_global_device_ids=true, to_apply=%region_25.0 | all-reduce | flops 1024 | bytes 8192 | tf_op jit(solution)/shard_map/psum | solution.py:22
  697.8 9.1 %fusion.11 = bf16[1024,1024]{1,0:T(8,128)(2,1)S(1)} fusion(bf16[2048,1024]{0,1:T(8,128)(2,1)} %all-gather.5.cloned.1.call-done, f32[1024,2048]{1,0:T(8,128)} %get-tuple-element.4, f32[1024]{0:T(1024)S(1)} %multiply_subtract_fusion.3, f32[2048]{0:T(1024)S(1)} %multiply_subtract_fusion), kind=kOutput, calls=%fused_computation.27 | convolution fusion | flops 4306501632 | bytes 14692352 | tf_op jit(solution)/shard_map/dot_general | solution.py:55
  707.0 2.6 copy.5
  709.6 29.2 %reduce-scatter.4.cloned.1.call-done = bf16[128,1024]{1,0:T(8,128)(2,1)} async-done(((bf16[1024,1024]{1,0:T(8,128)(2,1)}), bf16[128,1024]{1,0:T(8,128)(2,1)}) %reduce-scatter.4.cloned.1.call-update) | async-done | bytes 262160
  738.8 1.8 copy.6
  (16 shorter events, 1.6 us)
Async XLA Ops:
  7.2 36.7 %all-gather.3.cloned.1.call-start = ((), (), s32[]{:S(2)}) async-start(), calls=%async_computation.1 | async-start | bytes 2359296 | tf_op jit(solution)/shard_map/all_gather | solution.py:27
  7.9 118.4 %all-gather.5.cloned.1.call-start = ((), (), s32[]{:S(2)}) async-start(), calls=%async_computation.2 | async-start | bytes 4325376 | tf_op jit(solution)/shard_map/all_gather | solution.py:35
  8.6 730.1 %reduce-scatter.4.cloned.1.call-start = ((), (), s32[]{:S(2)}) async-start(), calls=%async_computation.3 | async-start | bytes 2359296
  637.0 60.8 %copy-start = (f32[2048]{0:T(1024)}, f32[2048]{0:T(1024)S(1)}, u32[]{:S(2)}) copy-start(f32[2048]{0:T(1024)S(1)} %multiply_subtract_fusion) | copy-start | bytes 24580
  697.8 9.1 %copy-start.1 = (f32[1024]{0:T(1024)}, f32[1024]{0:T(1024)S(1)}, u32[]{:S(2)}) copy-start(f32[1024]{0:T(1024)S(1)} %multiply_subtract_fusion.3) | copy-start | bytes 12292
Sparse Core Ops, SparseCore 0:
  9.8 33.9 all-gather.2
  46.4 79.8 all-gather.4
  709.7 29.0 reduce-scatter.3
where the time goes:
time: 749 us; the launch traced here: 747 us
  blocking collectives  508 us (68%)
  waiting for transfers between devices  146 us (19%)
  other arithmetic  54.1 us (7%)
  matrix products  20.3 us (3%)
  between operations  13.9 us (2%)
    pmax x3, blocking collectives, column_lse(): peak_value = lax.pmax(jnp.max(scaled, axis=0), 'noise')  177 us
    psum x3, blocking collectives, column_lse(): lax.psum(jnp.sum(jnp.exp(scaled - peak_value[None, :]), axis=0), 'noise')  171 us
    pmax x3, blocking collectives, row_lse(): peak_value = lax.pmax(jnp.max(scaled, axis=1), 'dp')  123 us
    all_gather x1, waiting for transfers between devices, local(): full_latents = lax.all_gather(latents, 'noise', axis=1, tiled=True)  80.4 us
    psum x3, blocking collectives, row_lse(): lax.psum(jnp.sum(jnp.exp(scaled - peak_value[:, None]), axis=1), 'dp')  37.3 us
    all_gather x1, waiting for transfers between devices, local(): rows_here = lax.all_gather(noise_batch, 'dp', axis=1, tiled=True)  35.2 us
    unnamed x4, waiting for transfers between devices  30.6 us
  transfers between devices with their start and end apart: 3, of which 3 were waited for; matrix products, arithmetic and copies ran while one was open for 0% of the time, Pallas kernels for 0%

commit v1 on v0

v1 whole, which is shorter than its diff:
```python
import math

import jax
import jax.numpy as jnp
from jax import lax
from jax.experimental import pallas as pl
from jax.experimental.pallas import tpu as pltpu
from jax.sharding import PartitionSpec as P

EPSILON = 0.01
NZ, NY, NX, NC = 8, 4, 4, 2
ROWS, COLS, D = 1024, 2048, 1024
NN, NM = 32768, 16384
A_COLS = 1280
LOG2E = math.log2(math.e)
NORM_SCALE = LOG2E / (EPSILON * D)
CROSS_SCALE = 2.0 * NORM_SCALE
STRIP = 256

BF = jnp.bfloat16
F32 = jnp.float32

GATHER = [
    ("Az", "p", 1), ("Az", "q", 1), ("Ay", "p", 1, 0), ("Ay", "q", 1, 0),
    ("Bz", "p", 1, 0), ("Bz", "q", 1, 0), ("By", "p", 1), ("By", "q", 1),
    ("Az", "p", 2), ("Ay", "p", 1, -1), ("Ay", "q", 1, -1), ("Az", "q", 2),
    ("Ay", "p", 1, 1), ("Ay", "q", 1, 1), ("Bz", "p", 2, 0), ("Bz", "q", 2, 0),
    ("Ay", "p", 2, 0), ("Bz", "p", 1, -1), ("Bz", "q", 1, -1), ("Bz", "p", 1, 1),
    ("Bz", "q", 1, 1), ("X", "p", 1), ("X", "q", 1), ("XS", 0), ("By", "p", 2), ("Az", "p", 3), ("Ay", "p", 1, -2),
    ("Ay", "q", 1, -2), ("Az", "q", 3), ("Ay", "p", 2, -1), ("Ay", "q", 1, 2),
    ("Bz", "p", 3, 0), ("Bz", "q", 3, 0), ("Ay", "p", 1, 2), ("Bz", "p", 2, -1),
    ("Bz", "q", 2, -1), ("Bz", "p", 2, 1), ("Bz", "q", 2, 1), ("X", "p", 2), ("XS", 1), ("XS", 2), ("Ay", "p", 2, 1),
    ("Bz", "q", 1, 2), ("Bz", "p", 1, 2), ("XS", 3), ("norm",), ("Ay", "p", 1, -3), ("Ay", "q", 1, -3),
    ("Az", "p", 4), ("Ay", "p", 2, -2), ("Ay", "q", 1, 3), ("dot", 0), ("Bz", "p", 4, 0),
    ("Bz", "q", 3, -1), ("Bz", "p", 3, -1), ("Ay", "p", 1, 3), ("Bz", "q", 3, 1),
    ("Bz", "p", 3, 1), ("Bz", "q", 2, 2), ("Bz", "p", 2, 2), ("Ay", "p", 2, 2), ("dot", 1),
    ("Bz", "p", 4, -1), ("Ay", "p", 2, -3), ("Ay", "q", 1, -4), ("Bz", "p", 4, 1),
    ("Ay", "p", 1, -4), ("Bz", "q", 3, 2), ("Bz", "p", 3, 2), ("dot", 2), ("Ay", "p", 2, 3),
    ("Ay", "p", 2, -4), ("Bz", "p", 4, 2),
]
DEPTH_PAIRS = ((0, -1), (1, -2), (2, -3), (3, -4))
KEYS = [e for e in GATHER if e[0] in ("Az", "Ay", "By", "Bz")]
SEM_OF = {k: i for i, k in enumerate(KEYS)}
XKEYS = [("X", "p", 1), ("X", "q", 1), ("X", "p", 2), ("XS", 0), ("XS", 1), ("XS", 2), ("XS", 3)]
XSEM_OF = {k: i for i, k in enumerate(XKEYS)}


def exp2(v):
    return jnp.exp2(v)


def kernel(noise_ref, lat_ref, row_out, col_out, tgt_out,
           lat_v, yt, xb, s_ref, e_ref, vy, sq, m_b, l_b, g_b, t_b, colw, roww,
           cx1, cx2, cx3, cs2, cs3, rx1, rx2, rx3, rs1, rs2, rs3,
           sib_s, sib_r, acc, far_s, far_r, near_s, near_r, mrg_s, mrg_r,
           in_sem, ysend, yrecv, xsend, xrecv, csend, crecv, rsend, rrecv, psend, precv, fsend, frecv):
    noise = lax.axis_index("noise")
    dp = lax.axis_index("dp")
    z, y = noise // NY, noise % NY
    x, c = dp // NC, dp % NC
    s = 1 - 2 * c

    def dev(zz, yy, xx, cc):
        return {"noise": zz * NY + yy, "dp": xx * NC + cc}

    def zat(k):
        return lax.rem(z + s * k + 2 * NZ, NZ)

    def yat(k):
        return lax.rem(y + s * k + 2 * NY, NY)

    def xat(k):
        return lax.rem(x + s * k + 2 * NX, NX)

    own_x = pl.multiple_of(dp * 128, 128)
    load_lat = pltpu.make_async_copy(lat_ref, lat_v, in_sem.at[0])
    load_x = pltpu.make_async_copy(noise_ref, xb.at[:, pl.ds(own_x, 128)], in_sem.at[1])
    load_lat.start()
    load_x.start()

    noise_peer = lambda k: lax.rem(noise + k, NZ * NY)
    dp_peer = lambda k: lax.rem(dp + k, NX * NC)
    barrier = pltpu.get_barrier_semaphore()
    for k in range(1, NZ * NY):
        pl.semaphore_signal(barrier, 1, device_id={"noise": noise_peer(k), "dp": dp})
    for k in range(1, NX * NC):
        pl.semaphore_signal(barrier, 1, device_id={"noise": noise, "dp": dp_peer(k)})

    def yrow(zz, yy):
        return pl.multiple_of(zz * 128 + yy * 32, 32)

    load_lat.wait()
    eye = (lax.broadcasted_iota(jnp.int32, (32, 32), 0) == lax.broadcasted_iota(jnp.int32, (32, 32), 1)).astype(F32).astype(BF)
    lat_t = lax.dot_general(eye, lat_v[...], (((1,), (1,)), ((), ())), preferred_element_type=F32)
    yt[pl.ds(yrow(z, y), 32), :] = lat_t.astype(BF)
    load_x.wait()
    pl.semaphore_wait(barrier, NZ * NY - 1 + NX * NC - 1)

    def xblk(xx, cc):
        return xb.at[:, pl.ds(pl.multiple_of((xx * NC + cc) * 128, 128), 128)]

    def sgn(pq):
        return 1 if pq == "p" else -1

    def desc(key):
        kind = key[0]
        if kind == "X":
            o = sgn(key[1])
            blk = xblk(xat(-o * (key[2] - 1)), c)
            to = dev(z, y, xat(o), c)
            sems = xsend, xrecv, XSEM_OF[key]
        elif kind == "XS":
            blk = xblk(xat((0, -1, 1, -2)[key[1]]), c)
            to = dev(z, y, x, 1 - c)
            sems = xsend, xrecv, XSEM_OF[key]
        else:
            o = sgn(key[1])
            if kind == "Az":
                blk = (zat(-o * (key[2] - 1)), y)
            elif kind == "Ay":
                blk = (zat(key[3]), yat(-o * (key[2] - 1)))
            elif kind == "By":
                blk = (z, yat(-o * (key[2] - 1)))
            else:
                blk = (zat(-o * (key[2] - 1)), yat(key[3]))
            cols = pl.ds(0, A_COLS) if kind[0] == "A" else pl.ds(A_COLS, COLS - A_COLS)
            blk = yt.at[pl.ds(yrow(*blk), 32), cols]
            to = dev(zat(o), y, x, c) if kind[1] == "z" else dev(z, yat(o), x, c)
            i = SEM_OF[key]
            return pltpu.make_async_remote_copy(
                src_ref=blk, dst_ref=blk, send_sem=ysend, recv_sem=yrecv.at[i],
                device_id=to, device_id_type=pl.DeviceIdType.MESH)
        i = sems[2]
        return pltpu.make_async_remote_copy(
            src_ref=blk, dst_ref=blk, send_sem=sems[0].at[i], recv_sem=sems[1].at[i],
            device_id=to, device_id_type=pl.DeviceIdType.MESH)

    def arrive(key):
        kind = key[0]
        if kind == "X":
            blk = xblk(xat(-sgn(key[1]) * key[2]), c)
            sem = xrecv.at[XSEM_OF[key]]
        elif kind == "XS":
            blk = xblk(xat((0, 1, -1, 2)[key[1]]), 1 - c)
            sem = xrecv.at[XSEM_OF[key]]
        else:
            o = sgn(key[1])
            if kind == "Az":
                blk = (zat(-o * key[2]), y)
            elif kind == "Ay":
                blk = (zat(key[3]), yat(-o * key[2]))
            elif kind == "By":
                blk = (z, yat(-o * key[2]))
            else:
                blk = (zat(-o * key[2]), yat(key[3]))
            cols = pl.ds(0, A_COLS) if kind[0] == "A" else pl.ds(A_COLS, COLS - A_COLS)
            blk = yt.at[pl.ds(yrow(*blk), 32), cols]
            sem = yrecv.at[SEM_OF[key]]
        pltpu.make_async_copy(blk, blk, sem).wait()

    def add_squares(blk_ref, first):
        v = blk_ref[...].astype(F32)
        sq[...] = v * v if first else sq[...] + v * v

    def depth_dot(pair, strip):
        cols = pl.ds(pl.multiple_of(strip * STRIP, STRIP), STRIP)
        rows = [pl.ds(pl.multiple_of(zat(k) * 128, 128), 128) for k in DEPTH_PAIRS[pair]]
        lhs = jnp.concatenate([xb[:, r] for r in rows], axis=1)
        rhs = jnp.concatenate([yt[r, cols] for r in rows], axis=0)
        return cols, CROSS_SCALE * jnp.dot(lhs, rhs, preferred_element_type=F32)

    def first_dot(strip, carry):
        cols, v = depth_dot(0, strip)
        a = m_b[...]
        s_ref[:, cols] = v + jnp.concatenate([a, a], axis=1)
        return carry

    def next_dot(pair):
        def body(strip, carry):
            cols, v = depth_dot(pair, strip)
            s_ref[:, cols] = s_ref[:, cols] + v
            return carry
        return body

    desc(("Az", "p", 1)).start()
    desc(("Az", "q", 1)).start()
    desc(("Ay", "p", 1, 0)).start()
    desc(("Ay", "q", 1, 0)).start()
    desc(("By", "p", 1)).start()
    desc(("By", "q", 1)).start()
    desc(("Bz", "p", 1, 0)).start()
    desc(("Bz", "q", 1, 0)).start()
    desc(("X", "p", 1)).start()
    desc(("X", "q", 1)).start()
    desc(("XS", 0)).start()
    add_squares(xblk(x, c), True)

    for key in GATHER:
        kind = key[0]
        if kind == "norm":
            m_b[...] = jnp.broadcast_to(-NORM_SCALE * jnp.sum(sq[...], axis=1, keepdims=True), (ROWS, 128))
            continue
        if kind == "dot":
            if key[1] == 0:
                lax.fori_loop(0, COLS // STRIP, first_dot, 0)
            else:
                lax.fori_loop(0, COLS // STRIP, next_dot(key[1]), 0)
            continue
        arrive(key)
        if kind == "Az":
            o = sgn(key[1])
            if key[2] < (4 if o == 1 else 3):
                desc(("Az", key[1], key[2] + 1)).start()
            desc(("Ay", "p", 1, -o * key[2])).start()
            desc(("Ay", "q", 1, -o * key[2])).start()
        elif kind == "Ay":
            if key[1] == "p" and key[2] == 1:
                desc(("Ay", "p", 2, key[3])).start()
        elif kind == "By":
            o = sgn(key[1])
            if key[1] == "p" and key[2] == 1:
                desc(("By", "p", 2)).start()
            yo = 2 if key[2] == 2 else -o
            desc(("Bz", "p", 1, yo)).start()
            desc(("Bz", "q", 1, yo)).start()
        elif kind == "Bz":
            if key[2] < (4 if key[1] == "p" else 3):
                desc(("Bz", key[1], key[2] + 1, key[3])).start()
        elif kind == "X":
            if key == ("X", "p", 1):
                desc(("X", "p", 2)).start()
            desc(("XS", {("p", 1): 1, ("q", 1): 2, ("p", 2): 3}[key[1:]])).start()
            add_squares(xblk(xat(-sgn(key[1]) * key[2]), c), False)
        elif kind == "XS":
            add_squares(xblk(xat((0, 1, -1, 2)[key[1]]), 1 - c), False)

    def last_dot(strip, carry):
        cols, v = depth_dot(3, strip)
        v = s_ref[:, cols] + v
        s_ref[:, cols] = v
        peak = jnp.max(jnp.max(v.reshape(ROWS // 8, 8, STRIP), axis=0), axis=0, keepdims=True)
        total = jnp.sum(jnp.sum(exp2(s_ref[:, cols] - peak).reshape(ROWS // 8, 8, STRIP), axis=0), axis=0, keepdims=True)
        lse = peak + jnp.log2(total)
        for h in range(STRIP // 128):
            colw[pl.ds(strip * (STRIP // 128) + h, 1), :] = lse[:, h * 128:(h + 1) * 128]
        return carry

    lax.fori_loop(0, COLS // STRIP, last_dot, 0)

    def to_all_noise(buf, i):
        for k in range(1, NZ * NY):
            pltpu.make_async_remote_copy(
                src_ref=buf.at[noise], dst_ref=buf.at[noise], send_sem=csend.at[i], recv_sem=crecv.at[i],
                device_id={"noise": noise_peer(k), "dp": dp}, device_id_type=pl.DeviceIdType.MESH).start()

    def from_all_noise(buf, i):
        part = buf.at[pl.ds(0, NZ * NY - 1)]
        pltpu.make_async_copy(part, part, crecv.at[i]).wait()

    def to_all_dp(buf, i):
        for k in range(1, NX * NC):
            pltpu.make_async_remote_copy(
                src_ref=buf.at[dp], dst_ref=buf.at[dp], send_sem=rsend.at[i], recv_sem=rrecv.at[i],
                device_id={"noise": noise, "dp": dp_peer(k)}, device_id_type=pl.DeviceIdType.MESH).start()

    def from_all_dp(buf, i):
        part = buf.at[pl.ds(0, NX * NC - 1)]
        pltpu.make_async_copy(part, part, rrecv.at[i]).wait()

    def row_of(ref, n):
        return jnp.concatenate([ref[k:k + 1, :] for k in range(n)], axis=1)

    def dense_into(ref, row, n):
        for k in range(n):
            ref[k:k + 1, :] = row[:, k * 128:(k + 1) * 128]

    def stacked(row):
        n = row.shape[1]
        hi = row.astype(BF).astype(F32)
        lo = row - hi
        i = lax.broadcasted_iota(jnp.int32, (16, n), 0)
        return jnp.where(i == 0, jnp.broadcast_to(hi, (16, n)), jnp.where(i == 1, jnp.broadcast_to(lo, (16, n)), 0.0)).astype(BF)

    def lse_of(buf):
        v = buf[...]
        peak = jnp.max(v, axis=0)
        return peak + jnp.log2(jnp.sum(exp2(v - peak[None]), axis=0))

    def spread(ref, out):
        for b in range(ROWS // 128):
            out[b * 128:(b + 1) * 128, :] = jnp.broadcast_to(ref[b:b + 1, :], (128, 128)).T

    cx1[noise] = colw[...]
    to_all_noise(cx1, 0)
    whole_y = yt.at[pl.ds(0, 992), :]
    pltpu.make_async_copy(whole_y, whole_y, ysend).wait()
    for i in range(len(XKEYS)):
        b = xblk(x, c)
        pltpu.make_async_copy(b, b, xsend.at[i]).wait()
    from_all_noise(cx1, 0)
    col1 = -math.log2(NM) - lse_of(cx1)
    colw[...] = col1

    col_row = row_of(colw, 16)

    def row_pass(i, carry):
        rows = pl.ds(pl.multiple_of(i * 32, 32), 32)
        v = s_ref[rows, :] + col_row
        peak = jnp.max(v, axis=1, keepdims=True)
        e = exp2(v - peak)
        total = jnp.sum(e, axis=1, keepdims=True)
        e_ref[rows, :] = e.astype(BF)
        m_b[rows, :] = jnp.broadcast_to(peak, (32, 128))
        l_b[rows, :] = jnp.broadcast_to(peak + jnp.log2(total), (32, 128))
        return carry

    lax.fori_loop(0, ROWS // 32, row_pass, 0)
    lane = lax.broadcasted_iota(jnp.int32, (128, 128), 1)
    for b in range(ROWS // 128):
        blk = pl.ds(b * 128, 128)
        t = jnp.where(lane == 0, m_b[blk, :], l_b[blk, :]).T
        roww[0, b:b + 1, :] = t[0:1, :]
        roww[1, b:b + 1, :] = t[1:2, :]
    rx1[dp] = roww[1]
    to_all_dp(rx1, 0)
    from_all_dp(rx1, 0)
    lse1 = lse_of(rx1)
    g = exp2(roww[0] - lse1)
    row1 = -math.log2(NN) - lse1
    roww[0] = g

    def col_sums(buf, stage, i, u):
        roww[1] = u
        q = jnp.dot(stacked(row_of(roww.at[1], 8)), e_ref[...], preferred_element_type=F32)
        dense_into(colw, q[0:1, :] + q[1:2, :], 16)
        stage[...] = colw[...]
        buf[noise] = stage[...].astype(BF)
        to_all_noise(buf, i)

    def row_sums(v, buf, i):
        colw[...] = v
        q = lax.dot_general(stacked(row_of(colw, 16)), e_ref[...], (((1,), (1,)), ((), ())), preferred_element_type=F32)
        dense_into(roww.at[1], q[0:1, :] + q[1:2, :], 8)
        buf[dp] = roww[1] * roww[0]
        to_all_dp(buf, i)

    col_sums(cx2, cs2, 1, g)
    spread(roww.at[0], g_b)
    norms = jnp.zeros((1, COLS), F32)
    def col_norm(i, carry):
        v = yt[pl.ds(pl.multiple_of(i * 32, 32), 32), :].astype(F32)
        return carry + jnp.sum((v * v).reshape(4, 8, COLS), axis=0)
    norms = jnp.sum(lax.fori_loop(0, D // 32, col_norm, jnp.zeros((8, COLS), F32)), axis=0, keepdims=True)
    dense_into(cs3, norms, 16)
    from_all_noise(cx2, 1)
    row_sums(1.0 / jnp.sum(cx2[...].astype(F32), axis=0), rx2, 1)
    from_all_dp(rx2, 1)
    t2 = jnp.sum(rx2[...], axis=0)

    col_sums(cx3, cs2, 2, roww[0] / t2)
    from_all_noise(cx3, 2)
    q3 = jnp.sum(cx3[...].astype(F32), axis=0)
    v3 = 1.0 / q3
    col_out[...] = (EPSILON / LOG2E) * (col1 + 2.0 - jnp.log2(q3) + NORM_SCALE * cs3[...])
    row_sums(v3, rx3, 2)
    v_row = row_of(colw, 16)

    def scale_latents(i, carry):
        rows = pl.ds(pl.multiple_of(i * 32, 32), 32)
        vy[rows, :] = (yt[rows, :].astype(F32) * v_row).astype(BF)
        return carry

    lax.fori_loop(0, D // 32, scale_latents, 0)

    half = pl.ds(0, ROWS // 2), pl.ds(ROWS // 2, ROWS // 2)
    right, left = dev(z, y, lax.rem(x + 1, NX), c), dev(z, y, lax.rem(x + NX - 1, NX), c)

    def rcopy(src, dst, i, to):
        return pltpu.make_async_remote_copy(
            src_ref=src, dst_ref=dst, send_sem=fsend.at[i], recv_sem=frecv.at[i],
            device_id=to, device_id_type=pl.DeviceIdType.MESH)

    def sib_copy(k):
        return pltpu.make_async_remote_copy(
            src_ref=sib_s.at[k], dst_ref=sib_r.at[k], send_sem=psend.at[k], recv_sem=precv.at[k],
            device_id=dev(z, y, x, 1 - c), device_id_type=pl.DeviceIdType.MESH)

    def weigh(k, step):
        xx = lax.rem(x + step, NX)
        w = vy.at[pl.ds(pl.multiple_of(xx * 256, 256), 256), :]

        def body(h, carry):
            rows = pl.ds(pl.multiple_of(h * 512, 512), 512)
            p = lax.dot_general(e_ref[rows, :], w[...], (((1,), (1,)), ((), ())), preferred_element_type=F32)
            gg = g_b[rows, :]
            lo, hi = p[:, :128] * gg, p[:, 128:] * gg
            acc[k, rows, :] = jnp.where(c == 0, lo, hi)
            sib_s[k, rows, :] = jnp.where(c == 0, hi, lo).astype(BF)
            return carry

        lax.fori_loop(0, 2, body, 0)
        sib_copy(k).start()

    def presum(k):
        sib_copy(k).wait_recv()
        return acc[k] + sib_r[k].astype(F32)

    weigh(0, 2)
    weigh(1, 1)
    far_s[...] = presum(0).astype(BF)
    far = [rcopy(far_s.at[half[0]], far_r.at[0], 0, right), rcopy(far_s.at[half[1]], far_r.at[1], 1, left)]
    for f in far:
        f.start()
    weigh(2, 3)
    acc[1] = presum(1)
    near_s[0] = acc[1, half[1], :].astype(BF)
    near0 = rcopy(near_s.at[0], near_r.at[0], 2, right)
    near0.start()
    weigh(3, 0)
    acc[2] = presum(2)
    near_s[1] = acc[2, half[0], :].astype(BF)
    near1 = rcopy(near_s.at[1], near_r.at[1], 3, left)
    near1.start()
    far[0].wait_recv()
    mrg_s[0] = (acc[1, half[0], :] + far_r[0].astype(F32)).astype(BF)
    mrg0 = rcopy(mrg_s.at[0], mrg_r.at[0], 4, right)
    mrg0.start()
    far[1].wait_recv()
    mrg_s[1] = (acc[2, half[1], :] + far_r[1].astype(F32)).astype(BF)
    mrg1 = rcopy(mrg_s.at[1], mrg_r.at[1], 5, left)
    mrg1.start()
    acc[3] = presum(3)
    from_all_dp(rx3, 2)
    t3 = jnp.sum(rx3[...], axis=0)
    row_out[...] = (EPSILON / LOG2E) * (row1 - 2.0 - jnp.log2(t3))
    roww[1] = 1.0 / t3
    spread(roww.at[1], t_b)
    near0.wait_recv()
    near1.wait_recv()
    mrg0.wait_recv()
    tgt_out[half[0], :] = ((acc[3, half[0], :] + near_r[1].astype(F32) + mrg_r[0].astype(F32)) * t_b[half[0], :]).astype(BF)
    mrg1.wait_recv()
    tgt_out[half[1], :] = ((acc[3, half[1], :] + near_r[0].astype(F32) + mrg_r[1].astype(F32)) * t_b[half[1], :]).astype(BF)

    for d in far + [near0, near1, mrg0, mrg1]:
        d.wait_send()
    for k in range(4):
        sib_copy(k).wait_send()
    for i, buf in enumerate((cx1, cx2, cx3)):
        part = buf.at[pl.ds(0, NZ * NY - 1)]
        pltpu.make_async_copy(part, part, csend.at[i]).wait()
    for i, buf in enumerate((rx1, rx2, rx3)):
        part = buf.at[pl.ds(0, NX * NC - 1)]
        pltpu.make_async_copy(part, part, rsend.at[i]).wait()


def local(noise_batch, latents):
    v = pltpu.VMEM
    dma = pltpu.SemaphoreType.DMA
    row, col, tgt = pl.pallas_call(
        kernel,
        out_shape=(
            jax.ShapeDtypeStruct((8, 128), F32),
            jax.ShapeDtypeStruct((16, 128), F32),
            jax.ShapeDtypeStruct((ROWS, 128), BF),
        ),
        in_specs=[pl.BlockSpec(memory_space=pl.ANY)] * 2,
        out_specs=[pl.BlockSpec(memory_space=pltpu.VMEM)] * 3,
        scratch_shapes=[
            v((COLS, 32), BF),
            v((D, COLS), BF),
            v((ROWS, D), BF),
            v((ROWS, COLS), F32),
            v((ROWS, COLS), BF),
            v((D, COLS), BF),
            v((ROWS, 128), F32),
            v((ROWS, 128), F32),
            v((ROWS, 128), F32),
            v((ROWS, 128), F32),
            v((ROWS, 128), F32),
            v((16, 128), F32),
            v((2, 8, 128), F32),
            v((32, 16, 128), F32),
            v((32, 16, 128), BF),
            v((32, 16, 128), BF),
            v((16, 128), F32),
            v((16, 128), F32),
            v((8, 8, 128), F32),
            v((8, 8, 128), F32),
            v((8, 8, 128), F32),
            v((8, 128), F32),
            v((8, 128), F32),
            v((8, 128), F32),
            v((4, ROWS, 128), BF),
            v((4, ROWS, 128), BF),
            v((4, ROWS, 128), F32),
            v((ROWS, 128), BF),
            v((2, ROWS // 2, 128), BF),
            v((2, ROWS // 2, 128), BF),
            v((2, ROWS // 2, 128), BF),
            v((2, ROWS // 2, 128), BF),
            v((2, ROWS // 2, 128), BF),
            dma((2,)),
            dma,
            dma((len(KEYS),)),
            dma((len(XKEYS),)),
            dma((len(XKEYS),)),
            dma((3,)),
            dma((3,)),
            dma((3,)),
            dma((3,)),
            dma((4,)),
            dma((4,)),
            dma((6,)),
            dma((6,)),
        ],
        compiler_params=pltpu.CompilerParams(
            collective_id=0, has_side_effects=True, vmem_limit_bytes=56 * 2**20),
        cost_estimate=pl.CostEstimate(flops=4 * ROWS * COLS * D, bytes_accessed=2**20, transcendentals=2 * ROWS * COLS),
    )(noise_batch, latents)
    return row.reshape(ROWS), col.reshape(COLS), tgt


def solution(mesh):
    in_specs = (P("noise", "dp"), P("dp", "noise"))
    out_specs = (P("noise"), P("dp"), P("noise", "dp"))
    return jax.shard_map(local, mesh=mesh, in_specs=in_specs, out_specs=out_specs, check_vma=False)
```

time: 749 us -> 109 us (0.15)
  blocking collectives: 508 us -> 0 us
  waiting for transfers between devices: 146 us -> 0 us
  Pallas kernels: 0 us -> 103 us
  other arithmetic: 54.1 us -> 0 us
  matrix products: 20.3 us -> 0 us
  between operations: 13.9 us -> 0.66 us
    pmax x6 -> x0, blocking collectives: 300 us -> none  [the longest x3 177 us: column_lse(): peak_value = lax.pmax(jnp.max(scaled, axis=0), 'noise')]
    psum x6 -> x0, blocking collectives: 208 us -> none  [the longest x3 171 us: column_lse(): lax.psum(jnp.sum(jnp.exp(scaled - peak_value[None, :]), axis=0), 'noise')]
    all_gather x2 -> x0, waiting for transfers between devices: 116 us -> none  [the longest x1 80.4 us: local(): full_latents = lax.all_gather(latents, 'noise', axis=1, tiled=True)]
    pallas_call x0 -> x1, Pallas kernels: none -> 103 us  [local(): pl.pallas_call(kernel, out_shape=(jax.ShapeDtypeStruct((8, 128), F32), ja...]
    reduce_sum x8 -> x0, other arithmetic: 32.7 us -> none  [the longest x3 14.1 us: column_lse(): jnp.sum(jnp.exp(scaled - peak_value[None, :]), axis=0)]
    unnamed x4 -> x0, waiting for transfers between devices: 30.6 us -> none
    reduce_max x5 -> x0, other arithmetic: 21.4 us -> none  [the longest x3 12.8 us: row_lse(): peak_value = lax.pmax(jnp.max(scaled, axis=1), 'dp')]
    dot_general x2 -> x0, matrix products: 20.3 us -> none  [the longest x1 11.1 us: local(): lax.dot_general(rows_here, full_latents, (((1,), (1,)), ((), ())), prefer...]
  transfers between devices with their start and end apart: 3 -> 0, of which waited for: 3 -> 0; matrix products, arithmetic and copies ran while one was open for 0% -> 0% of each run, Pallas kernels for 0% -> 0%
where the time goes in v1:
time: 109 us
  Pallas kernels  103 us (94%)
  local copies, waits for them, and re-layouts  5.43 us (5%)
    pallas_call x1, Pallas kernels, local(): pl.pallas_call(kernel, out_shape=(jax.ShapeDtypeStruct((8, 128), F32), ja...  103 us
    unnamed x8, local copies, waits for them, and re-layouts  5.43 us

profile of v1, /device:TPU:1, one launch (start us, length us, event | category | flops | bytes accessed | tf_op | source)
XLA Modules:
  0.0 109.1 jit_solution(9592141182465618532)
XLA Ops:
  0.6 1.9 %copy.5.lat_ref = bf16[2048,32]{1,0:T(8,128)(2,1)} copy(bf16[2048,32]{0,1:T(8,128)(2,1)} %param.3) | data formatting | bytes 262144 | tf_op args[1]
  2.5 103.0 %shard_map.49 = (f32[8,128]{1,0:T(8,128)}, f32[16,128]{1,0:T(8,128)}, bf16[1024,128]{1,0:T(8,128)(2,1)}) custom-call(bf16[1024,128]{1,0:T(8,128)(2,1)} %noise_ref.1, bf16[2048,32]{1,0:T(8,128)(2,1)} %copy.5.lat_ref), custom_call_target="tpu_custom_call" | custom-call | flops 8589934592 | bytes 1048576 | tf_op jit(solution)/shard_map/pallas_call | solution.py:460
  105.5 0.0 copy-start.1
  105.5 0.0 copy-start
  105.6 0.7 copy-done.1
  106.2 0.6 copy.9
  106.8 0.0 copy-done
  106.8 0.6 copy.10
  107.4 1.7 %copy.11 = bf16[1024,128]{1,0:T(8,128)(2,1)} copy(bf16[1024,128]{1,0:T(8,128)(2,1)} %get-tuple-element.14) | data formatting | bytes 524288
Async XLA Ops:
  105.5 0.7 copy-start.1
  105.5 1.3 %copy-start = (f32[16,128]{1,0:T(8,128)S(1)}, f32[16,128]{1,0:T(8,128)}, u32[]{:S(2)}) copy-start(f32[16,128]{1,0:T(8,128)} %get-tuple-element.7) | copy-start | bytes 24580

commit v2 on v1

--- a/solution.py
+++ b/solution.py
@@ -44,14 +44,18 @@
 XKEYS = [("X", "p", 1), ("X", "q", 1), ("X", "p", 2), ("XS", 0), ("XS", 1), ("XS", 2), ("XS", 3)]
 XSEM_OF = {k: i for i, k in enumerate(XKEYS)}
 
+FAR_FIRST = sorted(
+    ((dz, dy) for dz in range(-3, 5) for dy in range(-1, 3) if dz or dy),
+    key=lambda p: (-abs(p[0]) - abs(p[1]), p))
+
 
 def exp2(v):
     return jnp.exp2(v)
 
 
 def kernel(noise_ref, lat_ref, row_out, col_out, tgt_out,
-           lat_v, yt, xb, s_ref, e_ref, vy, sq, m_b, l_b, g_b, t_b, colw, roww,
-           cx1, cx2, cx3, cs2, cs3, rx1, rx2, rx3, rs1, rs2, rs3,
+           yt, xb, s_ref, e_ref, vy, sq, m_b, l_b, g_b, t_b, colw, roww,
+           cx1, cx2, cx3, cs2, cs3, rx1, rx2, rx3,
            sib_s, sib_r, acc, far_s, far_r, near_s, near_r, mrg_s, mrg_r,
            in_sem, ysend, yrecv, xsend, xrecv, csend, crecv, rsend, rrecv, psend, precv, fsend, frecv):
     noise = lax.axis_index("noise")
@@ -72,29 +76,31 @@
     def xat(k):
         return lax.rem(x + s * k + 2 * NX, NX)
 
+    def yrow(zz, yy):
+        return pl.multiple_of(zz * 128 + yy * 32, 32)
+
     own_x = pl.multiple_of(dp * 128, 128)
-    load_lat = pltpu.make_async_copy(lat_ref, lat_v, in_sem.at[0])
+    load_lat = pltpu.make_async_copy(lat_ref, yt.at[pl.ds(yrow(z, y), 32), :], in_sem.at[0])
     load_x = pltpu.make_async_copy(noise_ref, xb.at[:, pl.ds(own_x, 128)], in_sem.at[1])
     load_lat.start()
     load_x.start()
 
-    noise_peer = lambda k: lax.rem(noise + k, NZ * NY)
-    dp_peer = lambda k: lax.rem(dp + k, NX * NC)
+    MESH = pl.DeviceIdType.MESH
     barrier = pltpu.get_barrier_semaphore()
-    for k in range(1, NZ * NY):
-        pl.semaphore_signal(barrier, 1, device_id={"noise": noise_peer(k), "dp": dp})
-    for k in range(1, NX * NC):
-        pl.semaphore_signal(barrier, 1, device_id={"noise": noise, "dp": dp_peer(k)})
-
-    def yrow(zz, yy):
-        return pl.multiple_of(zz * 128 + yy * 32, 32)
+    around = [dev(zat(1), y, x, c), dev(zat(-1), y, x, c), dev(z, yat(1), x, c), dev(z, yat(-1), x, c),
+              dev(z, y, xat(1), c), dev(z, y, xat(-1), c), dev(z, y, x, 1 - c)]
+    for to in around:
+        pl.semaphore_signal(barrier, 1, device_id=to, device_id_type=MESH)
 
     load_lat.wait()
-    eye = (lax.broadcasted_iota(jnp.int32, (32, 32), 0) == lax.broadcasted_iota(jnp.int32, (32, 32), 1)).astype(F32).astype(BF)
-    lat_t = lax.dot_general(eye, lat_v[...], (((1,), (1,)), ((), ())), preferred_element_type=F32)
-    yt[pl.ds(yrow(z, y), 32), :] = lat_t.astype(BF)
     load_x.wait()
-    pl.semaphore_wait(barrier, NZ * NY - 1 + NX * NC - 1)
+    pl.semaphore_wait(barrier, len(around))
+
+    pending = []
+
+    def finish():
+        for part, sem in pending:
+            pltpu.make_async_copy(part, part, sem).wait()
 
     def xblk(xx, cc):
         return xb.at[:, pl.ds(pl.multiple_of((xx * NC + cc) * 128, 128), 128)]
@@ -234,6 +240,10 @@
         elif kind == "XS":
             add_squares(xblk(xat((0, 1, -1, 2)[key[1]]), 1 - c), False)
 
+    pending.append((yt.at[pl.ds(0, len(KEYS) // 2 * 32), :], ysend))
+    for i in range(len(XKEYS)):
+        pending.append((xblk(x, c), xsend.at[i]))
+
     def last_dot(strip, carry):
         cols, v = depth_dot(3, strip)
         v = s_ref[:, cols] + v
@@ -248,20 +258,22 @@
     lax.fori_loop(0, COLS // STRIP, last_dot, 0)
 
     def to_all_noise(buf, i):
-        for k in range(1, NZ * NY):
+        for dz, dy in FAR_FIRST:
             pltpu.make_async_remote_copy(
                 src_ref=buf.at[noise], dst_ref=buf.at[noise], send_sem=csend.at[i], recv_sem=crecv.at[i],
-                device_id={"noise": noise_peer(k), "dp": dp}, device_id_type=pl.DeviceIdType.MESH).start()
+                device_id=dev(zat(dz), yat(dy), x, c), device_id_type=MESH).start()
+        pending.append((buf.at[pl.ds(0, NZ * NY - 1)], csend.at[i]))
 
     def from_all_noise(buf, i):
         part = buf.at[pl.ds(0, NZ * NY - 1)]
         pltpu.make_async_copy(part, part, crecv.at[i]).wait()
 
     def to_all_dp(buf, i):
-        for k in range(1, NX * NC):
+        for dx, dc in ((2, 0), (2, 1), (1, 0), (1, 1), (-1, 0), (-1, 1), (0, 1)):
             pltpu.make_async_remote_copy(
                 src_ref=buf.at[dp], dst_ref=buf.at[dp], send_sem=rsend.at[i], recv_sem=rrecv.at[i],
-                device_id={"noise": noise, "dp": dp_peer(k)}, device_id_type=pl.DeviceIdType.MESH).start()
+                device_id=dev(z, y, xat(dx), 1 - c if dc else c), device_id_type=MESH).start()
+        pending.append((buf.at[pl.ds(0, NX * NC - 1)], rsend.at[i]))
 
     def from_all_dp(buf, i):
         part = buf.at[pl.ds(0, NX * NC - 1)]
@@ -292,35 +304,46 @@
 
     cx1[noise] = colw[...]
     to_all_noise(cx1, 0)
-    whole_y = yt.at[pl.ds(0, 992), :]
-    pltpu.make_async_copy(whole_y, whole_y, ysend).wait()
-    for i in range(len(XKEYS)):
-        b = xblk(x, c)
-        pltpu.make_async_copy(b, b, xsend.at[i]).wait()
     from_all_noise(cx1, 0)
     col1 = -math.log2(NM) - lse_of(cx1)
     colw[...] = col1
 
     col_row = row_of(colw, 16)
 
-    def row_pass(i, carry):
-        rows = pl.ds(pl.multiple_of(i * 32, 32), 32)
-        v = s_ref[rows, :] + col_row
-        peak = jnp.max(v, axis=1, keepdims=True)
-        e = exp2(v - peak)
-        total = jnp.sum(e, axis=1, keepdims=True)
-        e_ref[rows, :] = e.astype(BF)
-        m_b[rows, :] = jnp.broadcast_to(peak, (32, 128))
-        l_b[rows, :] = jnp.broadcast_to(peak + jnp.log2(total), (32, 128))
+    def lane_tiles(v):
+        return [v[:, k * 128:(k + 1) * 128] for k in range(COLS // 128)]
+
+    def tree(op, parts):
+        while len(parts) > 1:
+            parts = [op(*parts[i:i + 2]) for i in range(0, len(parts), 2)]
+        return parts[0]
+
+    def row_peaks(i, carry):
+        rows = pl.ds(pl.multiple_of(i * 16, 16), 16)
+        l_b[rows, :] = tree(jnp.maximum, lane_tiles(s_ref[rows, :] + col_row))
         return carry
 
-    lax.fori_loop(0, ROWS // 32, row_pass, 0)
-    lane = lax.broadcasted_iota(jnp.int32, (128, 128), 1)
+    lax.fori_loop(0, ROWS // 16, row_peaks, 0, unroll=4)
     for b in range(ROWS // 128):
         blk = pl.ds(b * 128, 128)
-        t = jnp.where(lane == 0, m_b[blk, :], l_b[blk, :]).T
-        roww[0, b:b + 1, :] = t[0:1, :]
-        roww[1, b:b + 1, :] = t[1:2, :]
+        t = l_b[blk, :]
+        m_b[blk, :] = jnp.broadcast_to(jnp.max(t, axis=1, keepdims=True), (128, 128))
+        roww[0, b:b + 1, :] = jnp.max(t.T, axis=0, keepdims=True)
+
+    def row_exps(i, carry):
+        rows = pl.ds(pl.multiple_of(i * 16, 16), 16)
+        peak = m_b[rows, :]
+        parts = [exp2(v - peak) for v in lane_tiles(s_ref[rows, :] + col_row)]
+        for k, e in enumerate(parts):
+            e_ref[rows, k * 128:(k + 1) * 128] = e.astype(BF)
+        l_b[rows, :] = tree(jnp.add, parts)
+        return carry
+
+    lax.fori_loop(0, ROWS // 16, row_exps, 0, unroll=4)
+    for b in range(ROWS // 128):
+        t = l_b[b * 128:(b + 1) * 128, :].T
+        roww[1, b:b + 1, :] = jnp.sum(t, axis=0, keepdims=True)
+    roww[1] = roww[0] + jnp.log2(roww[1])
     rx1[dp] = roww[1]
     to_all_dp(rx1, 0)
     from_all_dp(rx1, 0)
@@ -446,12 +469,13 @@
         d.wait_send()
     for k in range(4):
         sib_copy(k).wait_send()
-    for i, buf in enumerate((cx1, cx2, cx3)):
-        part = buf.at[pl.ds(0, NZ * NY - 1)]
-        pltpu.make_async_copy(part, part, csend.at[i]).wait()
-    for i, buf in enumerate((rx1, rx2, rx3)):
-        part = buf.at[pl.ds(0, NX * NC - 1)]
-        pltpu.make_async_copy(part, part, rsend.at[i]).wait()
+    finish()
+
+
+def place(row_in, col_in, tgt_in, row_out, col_out, tgt_out):
+    row_out[...] = row_in[...]
+    col_out[...] = col_in[...]
+    tgt_out[...] = tgt_in[...]
 
 
 def local(noise_batch, latents):
@@ -467,7 +491,6 @@
         in_specs=[pl.BlockSpec(memory_space=pl.ANY)] * 2,
         out_specs=[pl.BlockSpec(memory_space=pltpu.VMEM)] * 3,
         scratch_shapes=[
-            v((COLS, 32), BF),
             v((D, COLS), BF),
             v((ROWS, D), BF),
             v((ROWS, COLS), F32),
@@ -488,9 +511,6 @@
             v((8, 8, 128), F32),
             v((8, 8, 128), F32),
             v((8, 8, 128), F32),
-            v((8, 128), F32),
-            v((8, 128), F32),
-            v((8, 128), F32),
             v((4, ROWS, 128), BF),
             v((4, ROWS, 128), BF),
             v((4, ROWS, 128), F32),
@@ -517,7 +537,18 @@
         compiler_params=pltpu.CompilerParams(
             collective_id=0, has_side_effects=True, vmem_limit_bytes=56 * 2**20),
         cost_estimate=pl.CostEstimate(flops=4 * ROWS * COLS * D, bytes_accessed=2**20, transcendentals=2 * ROWS * COLS),
-    )(noise_batch, latents)
+    )(noise_batch, latents.T)
+    row, col, tgt = pl.pallas_call(
+        place,
+        out_shape=(
+            jax.ShapeDtypeStruct((8, 128), F32),
+            jax.ShapeDtypeStruct((16, 128), F32),
+            jax.ShapeDtypeStruct((ROWS, 128), BF),
+        ),
+        in_specs=[pl.BlockSpec(memory_space=pltpu.VMEM)] * 3,
+        out_specs=[pl.BlockSpec(memory_space=pltpu.VMEM)] * 3,
+        compiler_params=pltpu.CompilerParams(vmem_limit_bytes=60 * 2**20),
+    )(row, col, tgt)
     return row.reshape(ROWS), col.reshape(COLS), tgt
 
 

time: 109 us -> 96.7 us (0.89)
  Pallas kernels: 103 us -> 95.9 us
  local copies, waits for them, and re-layouts: 5.43 us -> 0 us
    pallas_call x1, Pallas kernels: 103 us -> 94.2 us  [local(): pl.pallas_call(kernel, out_shape=(jax.ShapeDtypeStruct((8, 128), F32), ja...]
    unnamed x8 -> x0, local copies, waits for them, and re-layouts: 5.43 us -> none
    pallas_call x0 -> x1, Pallas kernels: none -> 1.69 us  [local(): pl.pallas_call(place, out_shape=(jax.ShapeDtypeStruct((8, 128), F32), jax...]
where the time goes in v2:
time: 96.7 us; the launch traced here: 96.6 us
  Pallas kernels  95.9 us (99%)
    pallas_call x1, Pallas kernels, local(): pl.pallas_call(kernel, out_shape=(jax.ShapeDtypeStruct((8, 128), F32), ja...  94.2 us

profile of v2, /device:TPU:1, one launch (start us, length us, event | category | flops | bytes accessed | tf_op | source)
XLA Modules:
  0.0 96.6 jit_solution(1790237090568755952)
XLA Ops:
  0.6 94.2 %shard_map.49 = (f32[8,128]{1,0:T(8,128)}, f32[16,128]{1,0:T(8,128)}, bf16[1024,128]{1,0:T(8,128)(2,1)}) custom-call(bf16[1024,128]{1,0:T(8,128)(2,1)} %noise_ref.1, bf16[32,2048]{1,0:T(8,128)(2,1)} %bitcast.3), custom_call_target="tpu_custom_call" | custom-call | flops 8589934592 | bytes 1048576 | tf_op jit(solution)/shard_map/pallas_call | solution.py:484
  94.9 1.7 %shard_map.50 = (f32[8,128]{1,0:T(8,128)}, f32[16,128]{1,0:T(8,128)}, bf16[1024,128]{1,0:T(8,128)(2,1)}) custom-call(f32[8,128]{1,0:T(8,128)} %get-tuple-element.9.row_in, f32[16,128]{1,0:T(8,128)} %get-tuple-element.10.col_in, bf16[1024,128]{1,0:T(8,128)(2,1)} %get-tuple-element.11.tgt_in), custom_call_target="tpu_custom_call" | custom-call | tf_op jit(solution)/shard_map/pallas_call | solution.py:541

commit v3 on v2

v3 whole, which is shorter than its diff:
```python
import math

import jax
import jax.numpy as jnp
from jax import lax
from jax.experimental import pallas as pl
from jax.experimental.pallas import tpu as pltpu
from jax.sharding import PartitionSpec as P

EPSILON = 0.01
NZ, NY, NX, NC = 8, 4, 4, 2
ROWS, COLS, D = 1024, 2048, 1024
NN, NM = 32768, 16384
LOG2E = math.log2(math.e)
NORM_SCALE = LOG2E / (EPSILON * D)
CROSS_SCALE = 2.0 * NORM_SCALE
STRIP = 256

BF = jnp.bfloat16
F32 = jnp.float32

HELD_AT = {
    'Az': {('p', 1): 0, ('p', 2): 1, ('p', 3): 2, ('p', 4): 3, ('q', 1): 0, ('q', 2): 1, ('q', 3): 2},
    'By': {('p', 1): 0, ('q', 1): 0, ('p', 2): 1},
    'Ay': {('p', 1): 0, ('q', 1): 0, ('p', 2): 1},
    'Bz': {('p', 1): 0, ('p', 2): 1, ('p', 3): 2, ('p', 4): 3, ('q', 1): 0, ('q', 2): 1, ('q', 3): 2},
}
GROUPS = (('A', 0, 768), ('B', 768, 256), ('A', 1024, 512), ('B', 1536, 512))
GATHER = (
    ('go', 0), ('go', 1), ('go', 2), ('go', 3), ('XS', 0), ('Az', 0, 'p', 1), ('Az', 0, 'q', 1), ('Ay', 0, 'p', 1, 0),
    ('Ay', 0, 'q', 1, 0), ('Bz', 1, 'p', 1, 0), ('Bz', 1, 'q', 1, 0), ('By', 1, 'p', 1), ('By', 1, 'q', 1),
    ('Az', 2, 'p', 1), ('Az', 2, 'q', 1), ('Ay', 2, 'p', 1, 0), ('Ay', 2, 'q', 1, 0), ('Bz', 3, 'p', 1, 0),
    ('Bz', 3, 'q', 1, 0), ('By', 3, 'p', 1), ('By', 3, 'q', 1), ('Az', 0, 'p', 2), ('Ay', 0, 'p', 1, -1),
    ('Ay', 0, 'q', 1, -1), ('Az', 0, 'q', 2), ('Ay', 0, 'p', 1, 1), ('Ay', 0, 'q', 1, 1), ('Bz', 1, 'p', 2, 0),
    ('Bz', 1, 'q', 2, 0), ('Bz', 1, 'p', 1, -1), ('X', 'p', 1), ('Bz', 1, 'q', 1, -1), ('X', 'q', 1),
    ('Bz', 1, 'p', 1, 1), ('Ay', 0, 'p', 2, 0), ('Bz', 1, 'q', 1, 1), ('Az', 2, 'p', 2), ('Az', 2, 'q', 2),
    ('By', 1, 'p', 2), ('XS', 1), ('Bz', 3, 'p', 2, 0), ('Ay', 2, 'p', 1, -1), ('XS', 2), ('Ay', 2, 'q', 1, -1),
    ('Bz', 3, 'q', 2, 0), ('Bz', 3, 'p', 1, -1), ('Ay', 2, 'p', 1, 1), ('Ay', 2, 'q', 1, 1), ('Bz', 3, 'q', 1, -1),
    ('Bz', 3, 'p', 1, 1), ('Ay', 2, 'p', 2, 0), ('Bz', 3, 'q', 1, 1), ('By', 3, 'p', 2), ('Az', 0, 'p', 3),
    ('Ay', 0, 'p', 1, -2), ('Ay', 0, 'q', 1, -2), ('Az', 0, 'q', 3), ('Ay', 0, 'p', 2, -1), ('Ay', 0, 'q', 1, 2),
    ('Bz', 1, 'p', 3, 0), ('Bz', 1, 'q', 3, 0), ('Bz', 1, 'p', 2, -1), ('Bz', 1, 'q', 2, -1), ('Bz', 1, 'p', 2, 1),
    ('Ay', 0, 'p', 1, 2), ('Bz', 1, 'q', 2, 1), ('Az', 2, 'p', 3), ('Az', 2, 'q', 3), ('Ay', 0, 'p', 2, 1),
    ('Bz', 1, 'q', 1, 2), ('X', 'p', 2), ('Bz', 1, 'p', 1, 2), ('Bz', 3, 'p', 3, 0), ('Ay', 2, 'p', 1, -2),
    ('Ay', 2, 'q', 1, -2), ('Bz', 3, 'q', 3, 0), ('Bz', 3, 'p', 2, -1), ('Ay', 2, 'p', 1, 2), ('Ay', 2, 'q', 1, 2),
    ('Bz', 3, 'q', 2, -1), ('Bz', 3, 'p', 2, 1), ('Bz', 3, 'q', 2, 1), ('XS', 3), ('norm',), ('Ay', 2, 'p', 2, -1),
    ('Ay', 2, 'p', 2, 1), ('Bz', 3, 'q', 1, 2), ('Bz', 3, 'p', 1, 2), ('Ay', 0, 'p', 1, -3), ('Ay', 0, 'q', 1, -3),
    ('Ay', 0, 'p', 2, -2), ('Ay', 0, 'q', 1, 3), ('Az', 0, 'p', 4), ('Bz', 1, 'p', 4, 0), ('Bz', 1, 'q', 3, -1),
    ('Bz', 1, 'p', 3, -1), ('Ay', 0, 'p', 1, 3), ('Bz', 1, 'q', 3, 1), ('Bz', 1, 'p', 3, 1), ('Bz', 1, 'q', 2, 2),
    ('Az', 2, 'p', 4), ('Bz', 1, 'p', 2, 2), ('dot', 0, 0), ('Bz', 3, 'p', 4, 0), ('dot', 0, 1), ('Ay', 0, 'p', 2, 2),
    ('Bz', 3, 'q', 3, -1), ('Bz', 3, 'p', 3, -1), ('Ay', 2, 'p', 1, -3), ('Ay', 2, 'q', 1, -3), ('dot', 0, 2),
    ('Bz', 3, 'q', 3, 1), ('Bz', 3, 'p', 3, 1), ('Ay', 2, 'p', 1, 3), ('Ay', 2, 'q', 1, 3), ('Bz', 3, 'q', 2, 2),
    ('dot', 0, 3), ('Bz', 3, 'p', 2, 2), ('Ay', 2, 'p', 2, -2), ('Ay', 2, 'p', 2, 2), ('dot', 0, 4),
    ('Bz', 1, 'p', 4, -1), ('Bz', 1, 'p', 4, 1), ('Bz', 1, 'p', 3, 2), ('dot', 0, 5), ('Ay', 0, 'p', 2, -3),
    ('Ay', 0, 'q', 1, -4), ('Bz', 1, 'q', 3, 2), ('Ay', 0, 'p', 1, -4), ('dot', 0, 6), ('Bz', 3, 'p', 4, -1),
    ('Bz', 3, 'p', 4, 1), ('Ay', 0, 'p', 2, 3), ('dot', 0, 7), ('Bz', 3, 'q', 3, 2), ('Ay', 2, 'p', 1, -4),
    ('Bz', 3, 'p', 3, 2), ('Ay', 2, 'q', 1, -4), ('Ay', 2, 'p', 2, -3), ('Bz', 1, 'p', 4, 2), ('Ay', 2, 'p', 2, 3),
    ('Ay', 0, 'p', 2, -4), ('dot', 1, 0), ('Ay', 2, 'p', 2, -4), ('dot', 1, 1), ('Bz', 3, 'p', 4, 2), ('dot', 1, 2),
    ('dot', 1, 3), ('dot', 1, 4), ('dot', 1, 5), ('dot', 1, 6), ('dot', 1, 7),
)
DEPTHS = ((0, -1, 1, -2), (2, -3, 3, -4))
KEYS = [e for e in GATHER if e[0] in ("Az", "Ay", "By", "Bz")]
assert len(set(KEYS)) == len(KEYS) == 31 * len(GROUPS)
SEM_OF = {k: i for i, k in enumerate(KEYS)}
XKEYS = [("X", "p", 1), ("X", "q", 1), ("X", "p", 2), ("XS", 0), ("XS", 1), ("XS", 2), ("XS", 3)]
XSEM_OF = {k: i for i, k in enumerate(XKEYS)}

FAR_FIRST = sorted(
    ((dz, dy) for dz in range(-3, 5) for dy in range(-1, 3) if dz or dy),
    key=lambda p: (-abs(p[0]) - abs(p[1]), p))


def exp2(v):
    return jnp.exp2(v)


def kernel(noise_ref, lat_ref, row_out, col_out, tgt_out,
           yt, xb, s_ref, e_ref, vy, sq, m_b, l_b, g_b, t_b, colw, roww,
           cx1, cx2, cx3, cx4, cs2, cs3, rx1, rx2, rx3,
           sib_s, sib_r, acc, far_s, far_r, near_s, near_r, mrg_s, mrg_r,
           in_sem, ysend, yrecv, xsend, xrecv, csend, crecv, rsend, rrecv, psend, precv, fsend, frecv):
    noise = lax.axis_index("noise")
    dp = lax.axis_index("dp")
    z, y = noise // NY, noise % NY
    x, c = dp // NC, dp % NC
    s = 1 - 2 * c

    def dev(zz, yy, xx, cc):
        return {"noise": zz * NY + yy, "dp": xx * NC + cc}

    def zat(k):
        return lax.rem(z + s * k + 2 * NZ, NZ)

    def yat(k):
        return lax.rem(y + s * k + 2 * NY, NY)

    def xat(k):
        return lax.rem(x + s * k + 2 * NX, NX)

    def yrow(zz, yy):
        return pl.multiple_of(zz * 128 + yy * 32, 32)

    own_x = pl.multiple_of(dp * 128, 128)
    load_lat = pltpu.make_async_copy(lat_ref, yt.at[pl.ds(yrow(z, y), 32), :], in_sem.at[0])
    load_x = pltpu.make_async_copy(noise_ref, xb.at[:, pl.ds(own_x, 128)], in_sem.at[1])
    load_lat.start()
    load_x.start()

    MESH = pl.DeviceIdType.MESH
    barrier = pltpu.get_barrier_semaphore()
    around = [dev(zat(1), y, x, c), dev(zat(-1), y, x, c), dev(z, yat(1), x, c), dev(z, yat(-1), x, c),
              dev(z, y, xat(1), c), dev(z, y, xat(-1), c), dev(z, y, x, 1 - c)]
    for to in around:
        pl.semaphore_signal(barrier, 1, device_id=to, device_id_type=MESH)

    load_lat.wait()
    load_x.wait()
    pl.semaphore_wait(barrier, len(around))

    pending = []

    def finish():
        for part, sem in pending:
            pltpu.make_async_copy(part, part, sem).wait()

    def xblk(xx, cc):
        return xb.at[:, pl.ds(pl.multiple_of((xx * NC + cc) * 128, 128), 128)]

    def sgn(pq):
        return 1 if pq == "p" else -1

    def block(key, dist):
        kind, g, o = key[0], key[1], sgn(key[2])
        if kind == "Az":
            at = zat(-o * dist), y
        elif kind == "Ay":
            at = zat(key[4]), yat(-o * dist)
        elif kind == "By":
            at = z, yat(-o * dist)
        else:
            at = zat(-o * dist), yat(key[4])
        return yt.at[pl.ds(yrow(*at), 32), pl.ds(GROUPS[g][1], GROUPS[g][2])]

    def desc(key):
        kind = key[0]
        if kind == "X":
            o = sgn(key[1])
            blk = xblk(xat(-o * (key[2] - 1)), c)
            to = dev(z, y, xat(o), c)
            sems = xsend, xrecv, XSEM_OF[key]
        elif kind == "XS":
            blk = xblk(xat((0, -1, 1, -2)[key[1]]), c)
            to = dev(z, y, x, 1 - c)
            sems = xsend, xrecv, XSEM_OF[key]
        else:
            o = sgn(key[2])
            held = HELD_AT[kind][key[2:4]]
            blk = block(key, held)
            step = o * (key[3] - held)
            to = dev(zat(step), y, x, c) if kind[1] == "z" else dev(z, yat(step), x, c)
            return pltpu.make_async_remote_copy(
                src_ref=blk, dst_ref=blk, send_sem=ysend, recv_sem=yrecv.at[SEM_OF[key]],
                device_id=to, device_id_type=MESH)
        i = sems[2]
        return pltpu.make_async_remote_copy(
            src_ref=blk, dst_ref=blk, send_sem=sems[0].at[i], recv_sem=sems[1].at[i],
            device_id=to, device_id_type=pl.DeviceIdType.MESH)

    def arrive(key):
        kind = key[0]
        if kind == "X":
            blk = xblk(xat(-sgn(key[1]) * key[2]), c)
            sem = xrecv.at[XSEM_OF[key]]
        elif kind == "XS":
            blk = xblk(xat((0, 1, -1, 2)[key[1]]), 1 - c)
            sem = xrecv.at[XSEM_OF[key]]
        else:
            blk = block(key, key[3])
            sem = yrecv.at[SEM_OF[key]]
        pltpu.make_async_copy(blk, blk, sem).wait()

    def add_squares(blk_ref, first):
        v = blk_ref[...].astype(F32)
        sq[...] = v * v if first else sq[...] + v * v

    def dot_strip(half, strip):
        cols = pl.ds(pl.multiple_of(strip * STRIP, STRIP), STRIP)
        rows = [pl.ds(pl.multiple_of(zat(k) * 128, 128), 128) for k in DEPTHS[half]]
        lhs = jnp.concatenate([xb[:, r] for r in rows], axis=1)
        rhs = jnp.concatenate([yt[r, cols] for r in rows], axis=0)
        v = CROSS_SCALE * jnp.dot(lhs, rhs, preferred_element_type=F32)
        if half == 0:
            a = m_b[...]
            s_ref[:, cols] = v + jnp.concatenate([a, a], axis=1)
            return
        v = s_ref[:, cols] + v
        s_ref[:, cols] = v
        peak = jnp.max(jnp.max(v.reshape(ROWS // 8, 8, STRIP), axis=0), axis=0, keepdims=True)
        total = jnp.zeros((8, STRIP), F32)
        for r in range(0, ROWS, 256):
            e = exp2(s_ref[r:r + 256, cols] - peak)
            total = total + jnp.sum(e.reshape(32, 8, STRIP), axis=0)
        lse = peak + jnp.log2(jnp.sum(total, axis=0, keepdims=True))
        for h in range(STRIP // 128):
            colw[pl.ds(strip * (STRIP // 128) + h, 1), :] = lse[:, h * 128:(h + 1) * 128]

    def dense_into(ref, row, n):
        for k in range(n):
            ref[k:k + 1, :] = row[:, k * 128:(k + 1) * 128]

    def to_all_noise(buf, i):
        for dz, dy in FAR_FIRST:
            pltpu.make_async_remote_copy(
                src_ref=buf.at[noise], dst_ref=buf.at[noise], send_sem=csend.at[i], recv_sem=crecv.at[i],
                device_id=dev(zat(dz), yat(dy), x, c), device_id_type=MESH).start()

    def from_all_noise(buf, i):
        part = buf.at[pl.ds(0, NZ * NY - 1)]
        pltpu.make_async_copy(part, part, crecv.at[i]).wait()

    desc(("X", "p", 1)).start()
    desc(("X", "q", 1)).start()
    desc(("XS", 0)).start()
    add_squares(xblk(x, c), True)

    def send_on(kind, g, held, slot=(), only="pq"):
        for o in only:
            for (direction, dist), at in HELD_AT[kind].items():
                if direction == o and at == held:
                    desc((kind, g, o, dist) + slot).start()

    def handle(key):
        kind = key[0]
        if kind == "norm":
            m_b[...] = jnp.broadcast_to(-NORM_SCALE * jnp.sum(sq[...], axis=1, keepdims=True), (ROWS, 128))
            return
        if kind == "go":
            g = key[1]
            near, far = ("Az", "Ay") if GROUPS[g][0] == "A" else ("By", "Bz")
            send_on(near, g, 0)
            send_on(far, g, 0, (0,))
            return
        arrive(key)
        if kind in ("Az", "By"):
            g, pq, d = key[1:]
            send_on(kind, g, d, only=pq)
            if kind == "Az":
                send_on("Ay", g, 0, (-sgn(pq) * d,))
            else:
                send_on("Bz", g, 0, (2 if d == 2 else -sgn(pq),))
        elif kind in ("Ay", "Bz"):
            g, pq, d, slot = key[1:]
            send_on(kind, g, d, (slot,), only=pq)
        elif kind == "X":
            if key == ("X", "p", 1):
                desc(("X", "p", 2)).start()
            desc(("XS", {("p", 1): 1, ("q", 1): 2, ("p", 2): 3}[key[1:]])).start()
            add_squares(xblk(xat(-sgn(key[1]) * key[2]), c), False)
        elif kind == "XS":
            add_squares(xblk(xat((0, 1, -1, 2)[key[1]]), 1 - c), False)

    ahead, steps_now = [], []
    for key in GATHER:
        if key[0] == "dot":
            ahead.append((key[1:], steps_now))
            steps_now = []
        else:
            steps_now.append(key)
    strips = COLS // STRIP
    assert [k for k, _ in ahead] == [(h, i) for h in range(2) for i in range(strips)] and not steps_now

    for half_no in range(2):
        def strip_body(i, carry, half_no=half_no):
            for j in range(strips):
                todo = ahead[half_no * strips + j][1]
                if todo and (half_no, j) != (0, 0):
                    @pl.when(i == j)
                    def _():
                        for key in todo:
                            handle(key)
            if half_no:
                @pl.when(i == strips // 2)
                def _():
                    cx1[noise] = colw[0:8, :]
                    to_all_noise(cx1, 0)
            dot_strip(half_no, i)
            return carry

        if half_no == 0:
            for key in ahead[0][1]:
                handle(key)
        lax.fori_loop(0, strips, strip_body, 0)
    cx4[noise] = colw[8:16, :]
    to_all_noise(cx4, 3)
    pending.append((cx1.at[pl.ds(0, NZ * NY - 1)], csend.at[0]))
    pending.append((cx4.at[pl.ds(0, NZ * NY - 1)], csend.at[3]))
    pending.append((yt.at[pl.ds(0, (NZ * NY - 1) * 32), pl.ds(0, sum(g[2] for g in GROUPS))], ysend))
    for i in range(len(XKEYS)):
        pending.append((xblk(x, c), xsend.at[i]))

    def to_all_dp(buf, i):
        for dx, dc in ((2, 0), (2, 1), (1, 0), (1, 1), (-1, 0), (-1, 1), (0, 1)):
            pltpu.make_async_remote_copy(
                src_ref=buf.at[dp], dst_ref=buf.at[dp], send_sem=rsend.at[i], recv_sem=rrecv.at[i],
                device_id=dev(z, y, xat(dx), 1 - c if dc else c), device_id_type=MESH).start()
        pending.append((buf.at[pl.ds(0, NX * NC - 1)], rsend.at[i]))

    def from_all_dp(buf, i):
        part = buf.at[pl.ds(0, NX * NC - 1)]
        pltpu.make_async_copy(part, part, rrecv.at[i]).wait()

    def row_of(ref, n):
        return jnp.concatenate([ref[k:k + 1, :] for k in range(n)], axis=1)

    def stacked(row):
        n = row.shape[1]
        hi = row.astype(BF).astype(F32)
        lo = row - hi
        i = lax.broadcasted_iota(jnp.int32, (16, n), 0)
        return jnp.where(i == 0, jnp.broadcast_to(hi, (16, n)), jnp.where(i == 1, jnp.broadcast_to(lo, (16, n)), 0.0)).astype(BF)

    def lse_of(buf):
        v = buf[...]
        peak = jnp.max(v, axis=0)
        return peak + jnp.log2(jnp.sum(exp2(v - peak[None]), axis=0))

    def spread(ref, out):
        for b in range(ROWS // 128):
            out[b * 128:(b + 1) * 128, :] = jnp.broadcast_to(ref[b:b + 1, :], (128, 128)).T

    from_all_noise(cx1, 0)
    lse_a = lse_of(cx1)
    from_all_noise(cx4, 3)
    lse_b = lse_of(cx4)
    colw[0:8, :] = lse_a
    colw[8:16, :] = lse_b
    col1 = -math.log2(NM) - colw[...]
    colw[...] = col1

    col_row = row_of(colw, 16)

    def lane_tiles(v):
        return [v[:, k * 128:(k + 1) * 128] for k in range(COLS // 128)]

    def tree(op, parts):
        while len(parts) > 1:
            parts = [op(*parts[i:i + 2]) for i in range(0, len(parts), 2)]
        return parts[0]

    def row_peaks(i, carry):
        rows = pl.ds(pl.multiple_of(i * 16, 16), 16)
        l_b[rows, :] = tree(jnp.maximum, lane_tiles(s_ref[rows, :] + col_row))
        return carry

    lax.fori_loop(0, ROWS // 16, row_peaks, 0, unroll=4)
    for b in range(ROWS // 128):
        blk = pl.ds(b * 128, 128)
        t = l_b[blk, :]
        m_b[blk, :] = jnp.broadcast_to(jnp.max(t, axis=1, keepdims=True), (128, 128))
        roww[0, b:b + 1, :] = jnp.max(t.T, axis=0, keepdims=True)

    def row_exps(i, carry):
        rows = pl.ds(pl.multiple_of(i * 16, 16), 16)
        peak = m_b[rows, :]
        parts = [exp2(v - peak) for v in lane_tiles(s_ref[rows, :] + col_row)]
        for k, e in enumerate(parts):
            e_ref[rows, k * 128:(k + 1) * 128] = e.astype(BF)
        l_b[rows, :] = tree(jnp.add, parts)
        return carry

    lax.fori_loop(0, ROWS // 16, row_exps, 0, unroll=4)
    for b in range(ROWS // 128):
        t = l_b[b * 128:(b + 1) * 128, :].T
        roww[1, b:b + 1, :] = jnp.sum(t, axis=0, keepdims=True)
    roww[1] = roww[0] + jnp.log2(roww[1])
    rx1[dp] = roww[1]
    to_all_dp(rx1, 0)
    from_all_dp(rx1, 0)
    lse1 = lse_of(rx1)
    g = exp2(roww[0] - lse1)
    row1 = -math.log2(NN) - lse1
    roww[0] = g

    def col_sums(buf, stage, i, u):
        roww[1] = u
        q = jnp.dot(stacked(row_of(roww.at[1], 8)), e_ref[...], preferred_element_type=F32)
        dense_into(colw, q[0:1, :] + q[1:2, :], 16)
        stage[...] = colw[...]
        buf[noise] = stage[...].astype(BF)
        to_all_noise(buf, i)
        pending.append((buf.at[pl.ds(0, NZ * NY - 1)], csend.at[i]))

    def row_sums(v, buf, i):
        colw[...] = v
        q = lax.dot_general(stacked(row_of(colw, 16)), e_ref[...], (((1,), (1,)), ((), ())), preferred_element_type=F32)
        dense_into(roww.at[1], q[0:1, :] + q[1:2, :], 8)
        buf[dp] = roww[1] * roww[0]
        to_all_dp(buf, i)

    col_sums(cx2, cs2, 1, g)
    spread(roww.at[0], g_b)
    norms = jnp.zeros((1, COLS), F32)
    def col_norm(i, carry):
        v = yt[pl.ds(pl.multiple_of(i * 32, 32), 32), :].astype(F32)
        return carry + jnp.sum((v * v).reshape(4, 8, COLS), axis=0)
    norms = jnp.sum(lax.fori_loop(0, D // 32, col_norm, jnp.zeros((8, COLS), F32)), axis=0, keepdims=True)
    dense_into(cs3, norms, 16)
    from_all_noise(cx2, 1)
    row_sums(1.0 / jnp.sum(cx2[...].astype(F32), axis=0), rx2, 1)
    from_all_dp(rx2, 1)
    t2 = jnp.sum(rx2[...], axis=0)

    col_sums(cx3, cs2, 2, roww[0] / t2)
    from_all_noise(cx3, 2)
    q3 = jnp.sum(cx3[...].astype(F32), axis=0)
    v3 = 1.0 / q3
    col_out[...] = (EPSILON / LOG2E) * (col1 + 2.0 - jnp.log2(q3) + NORM_SCALE * cs3[...])
    colw[...] = v3
    v_row = row_of(colw, 16)

    half = pl.ds(0, ROWS // 2), pl.ds(ROWS // 2, ROWS // 2)
    right, left = dev(z, y, lax.rem(x + 1, NX), c), dev(z, y, lax.rem(x + NX - 1, NX), c)

    def rcopy(src, dst, i, to):
        return pltpu.make_async_remote_copy(
            src_ref=src, dst_ref=dst, send_sem=fsend.at[i], recv_sem=frecv.at[i],
            device_id=to, device_id_type=pl.DeviceIdType.MESH)

    def sib_copy(k, h):
        return pltpu.make_async_remote_copy(
            src_ref=sib_s.at[k, half[h]], dst_ref=sib_r.at[k, half[h]], send_sem=psend.at[2 * k + h], recv_sem=precv.at[2 * k + h],
            device_id=dev(z, y, x, 1 - c), device_id_type=MESH)

    def weigh(k, h):
        first = lax.rem(x + 2 + 3 * k + 3 * (k // 2) + 2 * (k // 3), NX) * 256

        @pl.when(h == 0)
        def _():
            def body(i, carry):
                rows = pl.ds(pl.multiple_of(first + i * 32, 32), 32)
                vy[rows, :] = (yt[rows, :].astype(F32) * v_row).astype(BF)
                return carry

            lax.fori_loop(0, 8, body, 0)

        w = vy[pl.ds(pl.multiple_of(first, 256), 256), :]
        rows = pl.ds(pl.multiple_of(h * (ROWS // 2), ROWS // 2), ROWS // 2)
        p = lax.dot_general(e_ref[rows, :], w, (((1,), (1,)), ((), ())), preferred_element_type=F32)
        gg = g_b[rows, :]
        lo, hi = p[:, :128] * gg, p[:, 128:] * gg
        acc[k, rows, :] = jnp.where(c == 0, lo, hi)
        sib_s[k, rows, :] = jnp.where(c == 0, hi, lo).astype(BF)

    def presum(k, h):
        sib_copy(k, h).wait_recv()
        return acc[k, half[h], :] + sib_r[k, half[h], :].astype(F32)

    far = [rcopy(far_s.at[half[0]], far_r.at[0], 0, right), rcopy(far_s.at[half[1]], far_r.at[1], 1, left)]
    near0 = rcopy(near_s.at[0], near_r.at[0], 2, right)
    near1 = rcopy(near_s.at[1], near_r.at[1], 3, left)
    mrg0 = rcopy(mrg_s.at[0], mrg_r.at[0], 4, right)
    mrg1 = rcopy(mrg_s.at[1], mrg_r.at[1], 5, left)
    def far_go(h):
        far_s[half[h], :] = presum(0, h).astype(BF)
        far[h].start()

    def near0_go():
        near_s[0] = presum(1, 1).astype(BF)
        near0.start()

    def near1_go():
        near_s[1] = presum(2, 0).astype(BF)
        near1.start()

    after = {2: lambda: far_go(0), 3: lambda: far_go(1), 4: near0_go, 5: near1_go}

    def weigh_body(i, carry):
        weigh(i // 2, i % 2)
        for j in range(8):
            @pl.when(i == j)
            def _():
                sib_copy(j // 2, j % 2).start()
                if j in after:
                    after[j]()
        return carry

    lax.fori_loop(0, 8, weigh_body, 0)
    row_sums(v3, rx3, 2)
    far[0].wait_recv()
    mrg_s[0] = (presum(1, 0) + far_r[0].astype(F32)).astype(BF)
    mrg0.start()
    far[1].wait_recv()
    mrg_s[1] = (presum(2, 1) + far_r[1].astype(F32)).astype(BF)
    mrg1.start()
    acc[3, half[0], :] = presum(3, 0)
    acc[3, half[1], :] = presum(3, 1)
    from_all_dp(rx3, 2)
    t3 = jnp.sum(rx3[...], axis=0)
    row_out[...] = (EPSILON / LOG2E) * (row1 - 2.0 - jnp.log2(t3))
    roww[1] = 1.0 / t3
    spread(roww.at[1], t_b)
    near0.wait_recv()
    near1.wait_recv()
    mrg0.wait_recv()
    tgt_out[half[0], :] = ((acc[3, half[0], :] + near_r[1].astype(F32) + mrg_r[0].astype(F32)) * t_b[half[0], :]).astype(BF)
    mrg1.wait_recv()
    tgt_out[half[1], :] = ((acc[3, half[1], :] + near_r[0].astype(F32) + mrg_r[1].astype(F32)) * t_b[half[1], :]).astype(BF)

    for d in far + [near0, near1, mrg0, mrg1]:
        d.wait_send()
    for k in range(4):
        for h in range(2):
            sib_copy(k, h).wait_send()
    finish()


def place(row_in, col_in, tgt_in, row_out, col_out, tgt_out):
    row_out[...] = row_in[...]
    col_out[...] = col_in[...]
    tgt_out[...] = tgt_in[...]


def local(noise_batch, latents):
    v = pltpu.VMEM
    dma = pltpu.SemaphoreType.DMA
    row, col, tgt = pl.pallas_call(
        kernel,
        out_shape=(
            jax.ShapeDtypeStruct((8, 128), F32),
            jax.ShapeDtypeStruct((16, 128), F32),
            jax.ShapeDtypeStruct((ROWS, 128), BF),
        ),
        in_specs=[pl.BlockSpec(memory_space=pl.ANY)] * 2,
        out_specs=[pl.BlockSpec(memory_space=pltpu.VMEM)] * 3,
        scratch_shapes=[
            v((D, COLS), BF),
            v((ROWS, D), BF),
            v((ROWS, COLS), F32),
            v((ROWS, COLS), BF),
            v((D, COLS), BF),
            v((ROWS, 128), F32),
            v((ROWS, 128), F32),
            v((ROWS, 128), F32),
            v((ROWS, 128), F32),
            v((ROWS, 128), F32),
            v((16, 128), F32),
            v((2, 8, 128), F32),
            v((32, 8, 128), F32),
            v((32, 16, 128), BF),
            v((32, 16, 128), BF),
            v((32, 8, 128), F32),
            v((16, 128), F32),
            v((16, 128), F32),
            v((8, 8, 128), F32),
            v((8, 8, 128), F32),
            v((8, 8, 128), F32),
            v((4, ROWS, 128), BF),
            v((4, ROWS, 128), BF),
            v((4, ROWS, 128), F32),
            v((ROWS, 128), BF),
            v((2, ROWS // 2, 128), BF),
            v((2, ROWS // 2, 128), BF),
            v((2, ROWS // 2, 128), BF),
            v((2, ROWS // 2, 128), BF),
            v((2, ROWS // 2, 128), BF),
            dma((2,)),
            dma,
            dma((len(KEYS),)),
            dma((len(XKEYS),)),
            dma((len(XKEYS),)),
            dma((4,)),
            dma((4,)),
            dma((3,)),
            dma((3,)),
            dma((8,)),
            dma((8,)),
            dma((6,)),
            dma((6,)),
        ],
        compiler_params=pltpu.CompilerParams(
            collective_id=0, has_side_effects=True, vmem_limit_bytes=56 * 2**20),
        cost_estimate=pl.CostEstimate(flops=4 * ROWS * COLS * D, bytes_accessed=2**20, transcendentals=2 * ROWS * COLS),
    )(noise_batch, latents.T)
    row, col, tgt = pl.pallas_call(
        place,
        out_shape=(
            jax.ShapeDtypeStruct((8, 128), F32),
            jax.ShapeDtypeStruct((16, 128), F32),
            jax.ShapeDtypeStruct((ROWS, 128), BF),
        ),
        in_specs=[pl.BlockSpec(memory_space=pltpu.VMEM)] * 3,
        out_specs=[pl.BlockSpec(memory_space=pltpu.VMEM)] * 3,
        compiler_params=pltpu.CompilerParams(vmem_limit_bytes=60 * 2**20),
    )(row, col, tgt)
    return row.reshape(ROWS), col.reshape(COLS), tgt


def solution(mesh):
    in_specs = (P("noise", "dp"), P("dp", "noise"))
    out_specs = (P("noise"), P("dp"), P("noise", "dp"))
    return jax.shard_map(local, mesh=mesh, in_specs=in_specs, out_specs=out_specs, check_vma=False)
```

time: 96.7 us -> 93.1 us (0.963)
  Pallas kernels: 95.9 us -> 92.3 us
    pallas_call x1, Pallas kernels: 94.2 us -> 90.6 us  [local(): pl.pallas_call(kernel, out_shape=(jax.ShapeDtypeStruct((8, 128), F32), ja...]
where the time goes in v3:
time: 93.1 us; the launch traced here: 93 us
  Pallas kernels  92.3 us (99%)
    pallas_call x1, Pallas kernels, local(): pl.pallas_call(kernel, out_shape=(jax.ShapeDtypeStruct((8, 128), F32), ja...  90.6 us

profile of v3, /device:TPU:1, one launch (start us, length us, event | category | flops | bytes accessed | tf_op | source)
XLA Modules:
  0.0 93.0 jit_solution(560581897864643604)
XLA Ops:
  0.6 90.6 %shard_map.49 = (f32[8,128]{1,0:T(8,128)}, f32[16,128]{1,0:T(8,128)}, bf16[1024,128]{1,0:T(8,128)(2,1)}) custom-call(bf16[1024,128]{1,0:T(8,128)(2,1)} %noise_ref.1, bf16[32,2048]{1,0:T(8,128)(2,1)} %bitcast.3), custom_call_target="tpu_custom_call" | custom-call | flops 8589934592 | bytes 1048576 | tf_op jit(solution)/shard_map/pallas_call | solution.py:525
  91.3 1.7 %shard_map.50 = (f32[8,128]{1,0:T(8,128)}, f32[16,128]{1,0:T(8,128)}, bf16[1024,128]{1,0:T(8,128)(2,1)}) custom-call(f32[8,128]{1,0:T(8,128)} %get-tuple-element.9.row_in, f32[16,128]{1,0:T(8,128)} %get-tuple-element.10.col_in, bf16[1024,128]{1,0:T(8,128)(2,1)} %get-tuple-element.11.tgt_in), custom_call_target="tpu_custom_call" | custom-call | tf_op jit(solution)/shard_map/pallas_call | solution.py:583

commit v4 on v3

--- a/solution.py
+++ b/solution.py
@@ -471,7 +471,7 @@
         near_s[1] = presum(2, 0).astype(BF)
         near1.start()
 
-    after = {2: lambda: far_go(0), 3: lambda: far_go(1), 4: near0_go, 5: near1_go}
+    after = {2: lambda: far_go(0), 3: lambda: far_go(1), 5: near0_go, 6: near1_go}
 
     def weigh_body(i, carry):
         weigh(i // 2, i % 2)

time: 93.1 us -> 91.2 us (0.980)
  Pallas kernels: 92.3 us -> 90.4 us
    pallas_call x1, Pallas kernels: 90.6 us -> 88.7 us  [local(): pl.pallas_call(kernel, out_shape=(jax.ShapeDtypeStruct((8, 128), F32), ja...]
where the time goes in v4:
time: 91.2 us; the launch traced here: 91.1 us
  Pallas kernels  90.4 us (99%)
    pallas_call x1, Pallas kernels, local(): pl.pallas_call(kernel, out_shape=(jax.ShapeDtypeStruct((8, 128), F32), ja...  88.7 us

profile of v4, /device:TPU:1, one launch (start us, length us, event | category | flops | bytes accessed | tf_op | source)
XLA Modules:
  0.0 91.1 jit_solution(6543259394523314596)
XLA Ops:
  0.6 88.7 %shard_map.49 = (f32[8,128]{1,0:T(8,128)}, f32[16,128]{1,0:T(8,128)}, bf16[1024,128]{1,0:T(8,128)(2,1)}) custom-call(bf16[1024,128]{1,0:T(8,128)(2,1)} %noise_ref.1, bf16[32,2048]{1,0:T(8,128)(2,1)} %bitcast.3), custom_call_target="tpu_custom_call" | custom-call | flops 8589934592 | bytes 1048576 | tf_op jit(solution)/shard_map/pallas_call | solution.py:525
  89.4 1.7 %shard_map.50 = (f32[8,128]{1,0:T(8,128)}, f32[16,128]{1,0:T(8,128)}, bf16[1024,128]{1,0:T(8,128)(2,1)}) custom-call(f32[8,128]{1,0:T(8,128)} %get-tuple-element.9.row_in, f32[16,128]{1,0:T(8,128)} %get-tuple-element.10.col_in, bf16[1024,128]{1,0:T(8,128)(2,1)} %get-tuple-element.11.tgt_in), custom_call_target="tpu_custom_call" | custom-call | tf_op jit(solution)/shard_map/pallas_call | solution.py:583

commit v5 on v4

--- a/solution.py
+++ b/solution.py
@@ -113,7 +113,6 @@
         pl.semaphore_signal(barrier, 1, device_id=to, device_id_type=MESH)
 
     load_lat.wait()
-    load_x.wait()
     pl.semaphore_wait(barrier, len(around))
 
     pending = []
@@ -216,11 +215,6 @@
     def from_all_noise(buf, i):
         part = buf.at[pl.ds(0, NZ * NY - 1)]
         pltpu.make_async_copy(part, part, crecv.at[i]).wait()
-
-    desc(("X", "p", 1)).start()
-    desc(("X", "q", 1)).start()
-    desc(("XS", 0)).start()
-    add_squares(xblk(x, c), True)
 
     def send_on(kind, g, held, slot=(), only="pq"):
         for o in only:
@@ -258,8 +252,18 @@
         elif kind == "XS":
             add_squares(xblk(xat((0, 1, -1, 2)[key[1]]), 1 - c), False)
 
+    for g in range(len(GROUPS)):
+        handle(("go", g))
+    load_x.wait()
+    desc(("X", "p", 1)).start()
+    desc(("X", "q", 1)).start()
+    desc(("XS", 0)).start()
+    add_squares(xblk(x, c), True)
+
     ahead, steps_now = [], []
     for key in GATHER:
+        if key[0] == "go":
+            continue
         if key[0] == "dot":
             ahead.append((key[1:], steps_now))
             steps_now = []

time: 91.2 us -> 91 us (level)
  no operation moved by 1% of the time
where the time goes in v5:
time: 91 us; the launch traced here: 90.9 us
  Pallas kernels  90.2 us (99%)
    pallas_call x1, Pallas kernels, local(): pl.pallas_call(kernel, out_shape=(jax.ShapeDtypeStruct((8, 128), F32), ja...  88.5 us

profile of v5, /device:TPU:1, one launch (start us, length us, event | category | flops | bytes accessed | tf_op | source)
XLA Modules:
  0.0 90.9 jit_solution(2808440948503458399)
XLA Ops:
  0.6 88.5 %shard_map.49 = (f32[8,128]{1,0:T(8,128)}, f32[16,128]{1,0:T(8,128)}, bf16[1024,128]{1,0:T(8,128)(2,1)}) custom-call(bf16[1024,128]{1,0:T(8,128)(2,1)} %noise_ref.1, bf16[32,2048]{1,0:T(8,128)(2,1)} %bitcast.3), custom_call_target="tpu_custom_call" | custom-call | flops 8589934592 | bytes 1048576 | tf_op jit(solution)/shard_map/pallas_call | solution.py:529
  89.2 1.7 %shard_map.50 = (f32[8,128]{1,0:T(8,128)}, f32[16,128]{1,0:T(8,128)}, bf16[1024,128]{1,0:T(8,128)(2,1)}) custom-call(f32[8,128]{1,0:T(8,128)} %get-tuple-element.9.row_in, f32[16,128]{1,0:T(8,128)} %get-tuple-element.10.col_in, bf16[1024,128]{1,0:T(8,128)(2,1)} %get-tuple-element.11.tgt_in), custom_call_target="tpu_custom_call" | custom-call | tf_op jit(solution)/shard_map/pallas_call | solution.py:587

commit v6 on v4

--- a/solution.py
+++ b/solution.py
@@ -351,7 +351,7 @@
         l_b[rows, :] = tree(jnp.maximum, lane_tiles(s_ref[rows, :] + col_row))
         return carry
 
-    lax.fori_loop(0, ROWS // 16, row_peaks, 0, unroll=4)
+    lax.fori_loop(0, ROWS // 16, row_peaks, 0, unroll=8)
     for b in range(ROWS // 128):
         blk = pl.ds(b * 128, 128)
         t = l_b[blk, :]
@@ -367,7 +367,7 @@
         l_b[rows, :] = tree(jnp.add, parts)
         return carry
 
-    lax.fori_loop(0, ROWS // 16, row_exps, 0, unroll=4)
+    lax.fori_loop(0, ROWS // 16, row_exps, 0, unroll=8)
     for b in range(ROWS // 128):
         t = l_b[b * 128:(b + 1) * 128, :].T
         roww[1, b:b + 1, :] = jnp.sum(t, axis=0, keepdims=True)

time: 91.2 us -> 91.1 us (level)
  no operation moved by 1% of the time
where the time goes in v6:
time: 91.1 us; the launch traced here: 91 us
  Pallas kernels  90.4 us (99%)
    pallas_call x1, Pallas kernels, local(): pl.pallas_call(kernel, out_shape=(jax.ShapeDtypeStruct((8, 128), F32), ja...  88.7 us

profile of v6, /device:TPU:1, one launch (start us, length us, event | category | flops | bytes accessed | tf_op | source)
XLA Modules:
  0.0 91.0 jit_solution(1836310426525226478)
XLA Ops:
  0.6 88.7 %shard_map.49 = (f32[8,128]{1,0:T(8,128)}, f32[16,128]{1,0:T(8,128)}, bf16[1024,128]{1,0:T(8,128)(2,1)}) custom-call(bf16[1024,128]{1,0:T(8,128)(2,1)} %noise_ref.1, bf16[32,2048]{1,0:T(8,128)(2,1)} %bitcast.3), custom_call_target="tpu_custom_call" | custom-call | flops 8589934592 | bytes 1048576 | tf_op jit(solution)/shard_map/pallas_call | solution.py:525
  89.3 1.7 %shard_map.50 = (f32[8,128]{1,0:T(8,128)}, f32[16,128]{1,0:T(8,128)}, bf16[1024,128]{1,0:T(8,128)(2,1)}) custom-call(f32[8,128]{1,0:T(8,128)} %get-tuple-element.9.row_in, f32[16,128]{1,0:T(8,128)} %get-tuple-element.10.col_in, bf16[1024,128]{1,0:T(8,128)(2,1)} %get-tuple-element.11.tgt_in), custom_call_target="tpu_custom_call" | custom-call | tf_op jit(solution)/shard_map/pallas_call | solution.py:583
